TPU v7x, 32 devices: a whole 2x2x4 slice. The times are simulated.
32 devices in a mesh: ctx: 8 (over z, y), tp: 4 (over x, core).
Axes of the slice: x: 2, y: 2, z: 4, core: 2. Of those that a mesh axis runs over, the one named last changes fastest.
Arguments:
- hidden_in: bfloat16 [2, 6656, 1024], P(None, ('ctx', 'tp')), may hold values from -6 to 6
- norm1_gain: float32 [1024], replicated, may hold values from 0.1 to 1.9
- qkv_weight: bfloat16 [1024, 3, 16, 64], P(None, None, 'tp'), may hold values from -0.1875 to 0.1875
- attn_weight: bfloat16 [16, 64, 1024], P('tp'), may hold values from -1 to 1
- norm2_gain: float32 [1024], replicated, may hold values from 0.1 to 1.9
- ffn_in_weight: bfloat16 [1024, 2, 2624], P(None, None, 'tp'), may hold values from -0.1875 to 0.1875
- ffn_out_weight: bfloat16 [2624, 1024], P('tp'), may hold values from -0.125 to 0.125
- doc_ids: int32 [2, 6656], P(None, 'ctx'), may hold values from 0 to 4, as said below
- out_grad: bfloat16 [2, 6656, 1024], P(None, ('ctx', 'tp')), may hold values from -6 to 6
Outputs:
- block_out: bfloat16 [2, 6656, 1024], P(None, ('ctx', 'tp'))
- in_grad: bfloat16 [2, 6656, 1024], P(None, ('ctx', 'tp'))
- norm1_gain_grad: float32 [1024], replicated
- qkv_weight_grad: float32 [1024, 3, 16, 64], P(None, None, 'tp')
- attn_weight_grad: float32 [16, 64, 1024], P('tp')
- norm2_gain_grad: float32 [1024], replicated
- ffn_in_weight_grad: float32 [1024, 2, 2624], P(None, None, 'tp')
- ffn_out_weight_grad: float32 [2624, 1024], P('tp')
Inputs may be any that keep to these rules, and one draw needn't show every extreme that they name: `doc_ids`: within each sequence the document numbers start at 0 and rise by one at each document start; one sequence, which one varying with the seed, is a single document over all 6656 tokens, and every other sequence holds exactly 5 documents.
All inputs are finite; a program needn't handle non-finite values.
Results may differ from a plain program's by a relative error of at most 0.024.
Values may be sent and summed in bfloat16 or wider, within the bound.
No kernel may reach another device: no remote copies, remote signals or barrier semaphores. Data moves between devices by JAX's collectives and lax.ppermute only.
A program may use at most 640 MiB of HBM per device.

v0:
```python
import math

import jax
import jax.numpy as jnp
from jax import lax
from jax.sharding import PartitionSpec as P

neg_fill = -1e30
theta_log = math.log(160000.0)


def from_behind(block, axis, distance):
    devices = range(lax.axis_size(axis))
    route = [((i - distance) % len(devices), i) for i in devices]
    return lax.ppermute(block, axis, route)


def rope_tables(positions, width):
    freqs = jnp.exp(-(2.0 * jnp.arange(width // 2, dtype=jnp.float32) / width) * theta_log)
    angles = positions.astype(jnp.float32)[:, None] * freqs[None, :]
    angles = jnp.concatenate([angles, angles], axis=1)
    return (jnp.cos(angles), jnp.sin(angles))


def rotate(values, cosine, sine):
    half = values.shape[-1] // 2
    turned = jnp.concatenate([-values[..., half:], values[..., :half]], axis=-1)
    return values * cosine[:, None, :] + turned * sine[:, None, :]


def unrotate(grads, cosine, sine):
    half = grads.shape[-1] // 2
    scaled = grads * sine[:, None, :]
    return grads * cosine[:, None, :] + jnp.concatenate(
        [scaled[..., half:], -scaled[..., :half]], axis=-1
    )


def layer_norm(rows, gain):
    mean = jnp.mean(rows, axis=-1, keepdims=True)
    cent = rows - mean
    var = jnp.mean(cent * cent, axis=-1, keepdims=True)
    return cent * lax.rsqrt(var + 1e-05) * gain


def shards(
    hidden_in,
    norm1_gain,
    qkv_weight,
    attn_weight,
    norm2_gain,
    ffn_in_weight,
    ffn_out_weight,
    doc_ids,
    out_grad,
):
    seqs = hidden_in.shape[0]
    width = hidden_in.shape[2]
    heads = qkv_weight.shape[2]
    head_dim = qkv_weight.shape[3]
    rows = doc_ids.shape[1]
    merged = heads * head_dim
    scale = 1.0 / math.sqrt(head_dim)
    cycle_size = lax.axis_size("ctx")
    me = lax.axis_index("ctx")
    all_seg = lax.all_gather(doc_ids, "ctx", axis=1, tiled=True)
    positions = me * rows + jnp.arange(rows, dtype=jnp.int32)
    cosine, sine = rope_tables(positions, head_dim)
    resid = hidden_in.astype(jnp.float32)
    normed1 = layer_norm(resid, norm1_gain).astype(jnp.bfloat16)
    full1 = lax.all_gather(normed1, "tp", axis=1, tiled=True)
    qkv = jnp.einsum("scd,dthe->scthe", full1, qkv_weight, preferred_element_type=jnp.float32)
    query = rotate(qkv[:, :, 0], cosine, sine).astype(jnp.bfloat16)
    key_rot = rotate(qkv[:, :, 1], cosine, sine).astype(jnp.bfloat16)
    value = qkv[:, :, 2].astype(jnp.bfloat16)
    kv_pair = jnp.stack([key_rot.reshape(seqs, rows, merged), value.reshape(seqs, rows, merged)])

    def score_block(pair, start):
        count = pair.shape[2]
        keys = pair[0].reshape(seqs, count, heads, head_dim)
        vals = pair[1].reshape(seqs, count, heads, head_dim)
        key_seg = lax.dynamic_slice_in_dim(all_seg, start, count, 1)
        allowed = doc_ids[:, None, :, None] == key_seg[:, None, None, :]
        scores = (
            jnp.einsum("sche,srhe->shcr", query, keys, preferred_element_type=jnp.float32) * scale
        )
        return (keys, vals, allowed, scores)

    run_max = jnp.full((seqs, heads, rows), neg_fill, jnp.float32)
    keys, vals, allowed, scores = score_block(
        lax.all_gather(kv_pair, "ctx", axis=2, tiled=True), jnp.int32(0)
    )
    new_max = jnp.maximum(run_max, jnp.max(jnp.where(allowed, scores, neg_fill), axis=-1))
    weights = jnp.where(allowed, jnp.exp(scores - new_max[..., None]), 0.0)
    run_sum = jnp.sum(weights, axis=-1)
    acc = jnp.einsum(
        "shcr,srhe->shce", weights.astype(jnp.bfloat16), vals, preferred_element_type=jnp.float32
    )
    run_max, run_sum, acc = (new_max, run_sum, acc)
    attn = acc / run_sum[..., None]
    lse = run_max + jnp.log(run_sum)
    attn_low = attn.transpose(0, 2, 1, 3).reshape(seqs, rows, merged).astype(jnp.bfloat16)
    attn_flat = attn_weight.reshape(merged, width)
    attn_sum = lax.psum_scatter(
        jnp.einsum("sck,kd->scd", attn_low, attn_flat, preferred_element_type=jnp.float32).astype(
            jnp.bfloat16
        ),
        "tp",
        scatter_dimension=1,
        tiled=True,
    ).astype(jnp.float32)
    mid = resid + attn_sum
    normed2 = layer_norm(mid, norm2_gain).astype(jnp.bfloat16)
    full2 = lax.all_gather(normed2, "tp", axis=1, tiled=True)
    upper = jnp.einsum("scd,dgf->scgf", full2, ffn_in_weight, preferred_element_type=jnp.float32)
    act = (jax.nn.gelu(upper[:, :, 0], approximate=False) * upper[:, :, 1]).astype(jnp.bfloat16)
    ffn_sum = lax.psum_scatter(
        jnp.einsum("scf,fd->scd", act, ffn_out_weight, preferred_element_type=jnp.float32).astype(
            jnp.bfloat16
        ),
        "tp",
        scatter_dimension=1,
        tiled=True,
    ).astype(jnp.float32)
    block_out = (mid + ffn_sum).astype(jnp.bfloat16)
    grad_full = lax.all_gather(out_grad, "tp", axis=1, tiled=True)
    d_act = jnp.einsum("scd,fd->scf", grad_full, ffn_out_weight, preferred_element_type=jnp.float32)
    grad_out_w = jnp.einsum("scf,scd->fd", act, grad_full, preferred_element_type=jnp.float32)
    _, pull_gelu = jax.vjp(
        lambda first, second: jax.nn.gelu(first, approximate=False) * second,
        upper[:, :, 0],
        upper[:, :, 1],
    )
    d_first, d_second = pull_gelu(d_act)
    d_upper = jnp.stack([d_first, d_second], axis=2).astype(jnp.bfloat16)
    grad_in_w = jnp.einsum("scd,scgf->dgf", full2, d_upper, preferred_element_type=jnp.float32)
    d_normed2 = lax.psum_scatter(
        jnp.einsum(
            "scgf,dgf->scd", d_upper, ffn_in_weight, preferred_element_type=jnp.float32
        ).astype(jnp.bfloat16),
        "tp",
        scatter_dimension=1,
        tiled=True,
    ).astype(jnp.float32)
    _, pull_norm2 = jax.vjp(layer_norm, mid, norm2_gain)
    d_mid_norm, grad_gain2 = pull_norm2(d_normed2)
    d_mid = out_grad.astype(jnp.float32) + d_mid_norm
    mid_full = lax.all_gather(d_mid.astype(jnp.bfloat16), "tp", axis=1, tiled=True)
    d_attn = (
        jnp.einsum("scd,kd->sck", mid_full, attn_flat, preferred_element_type=jnp.float32)
        .astype(jnp.bfloat16)
        .reshape(seqs, rows, heads, head_dim)
    )
    grad_attn_w = jnp.einsum(
        "sck,scd->kd", attn_low, mid_full, preferred_element_type=jnp.float32
    ).reshape(heads, head_dim, width)
    delta = jnp.sum(d_attn.astype(jnp.float32).transpose(0, 2, 1, 3) * attn, axis=-1)

    def back_block(pair, start):
        count = pair.shape[2]
        keys, vals, allowed, scores = score_block(pair, start)
        probs = jnp.where(allowed, jnp.exp(scores - lse[..., None]), 0.0)
        d_vals = jnp.einsum(
            "shcr,sche->srhe",
            probs.astype(jnp.bfloat16),
            d_attn,
            preferred_element_type=jnp.float32,
        )
        d_probs = jnp.einsum("sche,srhe->shcr", d_attn, vals, preferred_element_type=jnp.float32)
        d_scores = (probs * (d_probs - delta[..., None])).astype(jnp.bfloat16)
        add_query = (
            jnp.einsum("shcr,srhe->sche", d_scores, keys, preferred_element_type=jnp.float32)
            * scale
        )
        d_keys = (
            jnp.einsum("shcr,sche->srhe", d_scores, query, preferred_element_type=jnp.float32)
            * scale
        )
        return (
            add_query,
            jnp.stack([d_keys.reshape(seqs, count, merged), d_vals.reshape(seqs, count, merged)]),
        )

    query_zero = jnp.zeros((seqs, rows, heads, head_dim), jnp.float32)

    def cycle_turn(step, state):
        pair, d_pair, d_query = state
        owner = (me - step) % cycle_size
        add_query, add_pair = back_block(pair, owner * rows)
        pair = from_behind(pair, "ctx", 1)
        d_pair = from_behind((d_pair + add_pair).astype(jnp.bfloat16), "ctx", 1).astype(jnp.float32)
        return (pair, d_pair, d_query + add_query)

    _, d_kv, d_query = lax.fori_loop(
        0, cycle_size, cycle_turn, (kv_pair, jnp.zeros(kv_pair.shape, jnp.float32), query_zero)
    )
    d_keys = d_kv[0].reshape(seqs, rows, heads, head_dim)
    d_vals = d_kv[1].reshape(seqs, rows, heads, head_dim)
    d_qkv = jnp.stack(
        [unrotate(d_query, cosine, sine), unrotate(d_keys, cosine, sine), d_vals], axis=2
    ).astype(jnp.bfloat16)
    grad_qkv_w = jnp.einsum("scd,scthe->dthe", full1, d_qkv, preferred_element_type=jnp.float32)
    d_normed1 = lax.psum_scatter(
        jnp.einsum("scthe,dthe->scd", d_qkv, qkv_weight, preferred_element_type=jnp.float32).astype(
            jnp.bfloat16
        ),
        "tp",
        scatter_dimension=1,
        tiled=True,
    ).astype(jnp.float32)
    _, pull_norm1 = jax.vjp(layer_norm, resid, norm1_gain)
    d_in_norm, grad_gain1 = pull_norm1(d_normed1)
    in_grad = (d_mid + d_in_norm).astype(jnp.bfloat16)
    summed = (
        lax.psum(grad_qkv_w.astype(jnp.bfloat16), "ctx").astype(jnp.float32),
        lax.psum(grad_attn_w.astype(jnp.bfloat16), "ctx").astype(jnp.float32),
        lax.psum(grad_in_w.astype(jnp.bfloat16), "ctx").astype(jnp.float32),
        lax.psum(grad_out_w.astype(jnp.bfloat16), "ctx").astype(jnp.float32),
        lax.psum(grad_gain1.astype(jnp.bfloat16), "ctx").astype(jnp.float32),
        lax.psum(grad_gain2.astype(jnp.bfloat16), "ctx").astype(jnp.float32),
    )
    gains = lax.psum((summed[4], summed[5]), "tp")
    return (block_out, in_grad, gains[0], summed[0], summed[1], gains[1], summed[2], summed[3])


def solution(mesh):
    in_specs = (
        P(None, ("ctx", "tp"), None),
        P(),
        P(None, None, "tp", None),
        P("tp", None, None),
        P(),
        P(None, None, "tp"),
        P("tp", None),
        P(None, "ctx"),
        P(None, ("ctx", "tp"), None),
    )
    out_specs = (
        P(None, ("ctx", "tp"), None),
        P(None, ("ctx", "tp"), None),
        P(),
        P(None, None, "tp", None),
        P("tp", None, None),
        P(),
        P(None, None, "tp"),
        P("tp", None),
    )
    return jax.shard_map(shards, mesh=mesh, in_specs=in_specs, out_specs=out_specs, check_vma=False)
```

profile of v0, /device:TPU:0, one launch (start us, length us, event | category | flops | bytes accessed | tf_op | source)
XLA Modules:
  0.0 2188.8 jit_solution(14233497667411691785)
XLA Ops:
  21.3 25.5 %all-gather.7.cloned.1.call-done = bf16[2,832,1024]{2,1,0:T(8,128)(2,1)} async-done(((bf16[2,208,1024]{2,1,0:T(8,128)(2,1)}), bf16[2,832,1024]{2,1,0:T(8,128)(2,1)}) %all-gather.7.cloned.1.call-update) | async-done | bytes 3407888 | tf_op jit(solution)/shard_map/all_gather | solution.py:71
  75.3 31.2 %all-gather = s32[8,832,2]{1,2,0:T(2,128)S(1)} all-gather(s32[1,832,2]{1,2,0:T(2,128)S(1)} %bitcast.317), channel_id=1, replica_groups=mesh['ctx'=8,'tp'=4] {'ctx'}, dimensions={0}, use_global_device_ids=true | all-gather | bytes 59904 | tf_op jit(solution)/shard_map/all_gather | solution.py:66
  117.2 147.6 %all-gather.9.cloned.1.call-done = bf16[2,2,6656,256]{3,1,0,2:T(2,128)(2,1)} async-done(((bf16[2,2,832,256]{3,1,0,2:T(2,128)(2,1)}), bf16[2,2,6656,256]{3,1,0,2:T(2,128)(2,1)}) %all-gather.9.cloned.1.call-update) | async-done | bytes 13631504 | tf_op jit(solution)/shard_map/all_gather | solution.py:91
  276.8 17.4 copy.99
  294.2 66.8 %select_reduce_fusion = (f32[2,4,832]{2,1,0:T(4,128)S(1)}, f32[2,4,832,6656]{3,2,1,0:T(8,128)}) fusion(pred[2,832,6656]{2,1,0:T(8,128)(4,1)} %broadcast_compare_fusion.1, bf16[2,832,4,64]{1,3,2,0:T(8,128)(2,1)} %fusion.63, bf16[2,6656,4,64]{1,3,2,0:T(8,128)(2,1)} %bitcast.309), kind=kOutput, calls=%fused_computation.14 | convolution fusion | flops 5803599360 | bytes 195979264 | tf_op jit(solution)/shard_map/sche,srhe->shcr/dot_general | solution.py:85
  361.0 17.4 copy.100
  378.5 77.8 %fusion.7 = f32[2,4,832]{2,1,0:T(4,128)} fusion(f32[2,4,832,6656]{3,2,1,0:T(8,128)} %get-tuple-element.394, f32[2,4,832]{2,1,0:T(4,128)S(1)} %broadcast_maximum_fusion, pred[2,832,6656]{2,1,0:T(8,128)(4,1)} %broadcast_compare_fusion.1), kind=kLoop, calls=%fused_computation.15 | loop fusion | flops 177202688 | bytes 188338176 | tf_op jit(solution)/shard_map/reduce_sum | solution.py:95
  456.3 63.4 %fusion.9 = f32[2,4,832,64]{2,3,1,0:T(8,128)} fusion(bf16[2,6656,4,64]{1,3,2,0:T(8,128)(2,1)} %bitcast.308, f32[2,4,832,6656]{3,2,1,0:T(8,128)} %get-tuple-element.394, f32[2,4,832]{2,1,0:T(4,128)S(1)} %broadcast_maximum_fusion, pred[2,832,6656]{2,1,0:T(8,128)(4,1)} %broadcast_compare_fusion.1), kind=kOutput, calls=%fused_computation.17 | convolution fusion | flops 5847908352 | bytes 196831232 | tf_op jit(solution)/shard_map/shcr,srhe->shce/dot_general | solution.py:96
  524.7 37.3 %reduce-scatter.5.cloned.1.call-done = bf16[2,208,1024]{2,1,0:T(8,128)(2,1)} async-done(((bf16[2,832,1024]{2,1,0:T(8,128)(2,1)}), bf16[2,208,1024]{2,1,0:T(8,128)(2,1)}) %reduce-scatter.5.cloned.1.call-update) | async-done | bytes 851984 | tf_op jit(solution)/shard_map/reduce_scatter | solution.py:104
  566.6 27.0 %all-gather.13.cloned.1.call-done = bf16[2,832,1024]{2,1,0:T(8,128)(2,1)} async-done(((bf16[2,208,1024]{2,1,0:T(8,128)(2,1)}), bf16[2,832,1024]{2,1,0:T(8,128)(2,1)}) %all-gather.13.cloned.1.call-update) | async-done | bytes 3407888 | tf_op jit(solution)/shard_map/all_gather | solution.py:126
  600.8 25.0 %all-gather.11.cloned.1.call-done = bf16[2,832,1024]{2,1,0:T(8,128)(2,1)} async-done(((bf16[2,208,1024]{2,1,0:T(8,128)(2,1)}), bf16[2,832,1024]{2,1,0:T(8,128)(2,1)}) %all-gather.11.cloned.1.call-update) | async-done | bytes 3407888 | tf_op jit(solution)/shard_map/all_gather | solution.py:114
  655.3 39.7 %reduce-scatter.9.cloned.1.call-done = bf16[2,208,1024]{2,1,0:T(8,128)(2,1)} async-done(((bf16[2,832,1024]{2,1,0:T(8,128)(2,1)}), bf16[2,208,1024]{2,1,0:T(8,128)(2,1)}) %reduce-scatter.9.cloned.1.call-update) | async-done | bytes 851984 | tf_op jit(solution)/shard_map/reduce_scatter | solution.py:137
  736.5 1126.0 %while.20 = (s32[]{:T(128)}, bf16[2,2,832,256]{3,2,1,0:T(8,128)(2,1)}, f32[2,2,832,256]{3,2,1,0:T(8,128)}, f32[2,832,4,64]{1,3,2,0:T(8,128)}, s32[2,832]{1,0:T(2...) while((s32[]{:T(128)}, ...), condition=%wide.region_13.14_spmd.clone, body=%wide.region_12.13_spmd.clone.sunk | while | flops 3606913024 | bytes 166560176 | solution.py:194
  813.1 30.8 %collective-permute-done.1 = bf16[2,2,832,256]{3,2,1,0:T(8,128)(2,1)} collective-permute-done((bf16[2,2,832,256]{3,2,1,0:T(8,128)(2,1)}, bf16[2,2,832,256]{3,2,1,0:T(8,128)(2,1)}, u32[]{:S(2)}, u32[]{:S(2)}) %collective-permute-start.1) | collective-permute-done | bytes 1703968 | tf_op jit(solution)/shard_map/while/body/eval_jaxpr/ppermute | solution.py:15
  847.5 32.3 %collective-permute-done = bf16[2,2,832,256]{3,2,1,0:T(8,128)(2,1)} collective-permute-done((bf16[2,2,832,256]{3,2,1,0:T(8,128)(2,1)S(1)}, bf16[2,2,832,256]{3,2,1,0:T(8,128)(2,1)}, u32[]{:S(2)}, u32[]{:S(2)}) %collective-permute-start) | collective-permute-done | bytes 1703968 | tf_op jit(solution)/shard_map/while/body/eval_jaxpr/ppermute | solution.py:15
  955.8 32.2 %collective-permute-done.1 = bf16[2,2,832,256]{3,2,1,0:T(8,128)(2,1)} collective-permute-done((bf16[2,2,832,256]{3,2,1,0:T(8,128)(2,1)}, bf16[2,2,832,256]{3,2,1,0:T(8,128)(2,1)}, u32[]{:S(2)}, u32[]{:S(2)}) %collective-permute-start.1) | collective-permute-done | bytes 1703968 | tf_op jit(solution)/shard_map/while/body/eval_jaxpr/ppermute | solution.py:15
  991.5 31.4 %collective-permute-done = bf16[2,2,832,256]{3,2,1,0:T(8,128)(2,1)} collective-permute-done((bf16[2,2,832,256]{3,2,1,0:T(8,128)(2,1)S(1)}, bf16[2,2,832,256]{3,2,1,0:T(8,128)(2,1)}, u32[]{:S(2)}, u32[]{:S(2)}) %collective-permute-start) | collective-permute-done | bytes 1703968 | tf_op jit(solution)/shard_map/while/body/eval_jaxpr/ppermute | solution.py:15
  1097.8 33.4 %collective-permute-done.1 = bf16[2,2,832,256]{3,2,1,0:T(8,128)(2,1)} collective-permute-done((bf16[2,2,832,256]{3,2,1,0:T(8,128)(2,1)}, bf16[2,2,832,256]{3,2,1,0:T(8,128)(2,1)}, u32[]{:S(2)}, u32[]{:S(2)}) %collective-permute-start.1) | collective-permute-done | bytes 1703968 | tf_op jit(solution)/shard_map/while/body/eval_jaxpr/ppermute | solution.py:15
  1134.7 30.5 %collective-permute-done = bf16[2,2,832,256]{3,2,1,0:T(8,128)(2,1)} collective-permute-done((bf16[2,2,832,256]{3,2,1,0:T(8,128)(2,1)S(1)}, bf16[2,2,832,256]{3,2,1,0:T(8,128)(2,1)}, u32[]{:S(2)}, u32[]{:S(2)}) %collective-permute-start) | collective-permute-done | bytes 1703968 | tf_op jit(solution)/shard_map/while/body/eval_jaxpr/ppermute | solution.py:15
  1240.0 33.4 %collective-permute-done.1 = bf16[2,2,832,256]{3,2,1,0:T(8,128)(2,1)} collective-permute-done((bf16[2,2,832,256]{3,2,1,0:T(8,128)(2,1)}, bf16[2,2,832,256]{3,2,1,0:T(8,128)(2,1)}, u32[]{:S(2)}, u32[]{:S(2)}) %collective-permute-start.1) | collective-permute-done | bytes 1703968 | tf_op jit(solution)/shard_map/while/body/eval_jaxpr/ppermute | solution.py:15
  1276.9 29.6 %collective-permute-done = bf16[2,2,832,256]{3,2,1,0:T(8,128)(2,1)} collective-permute-done((bf16[2,2,832,256]{3,2,1,0:T(8,128)(2,1)S(1)}, bf16[2,2,832,256]{3,2,1,0:T(8,128)(2,1)}, u32[]{:S(2)}, u32[]{:S(2)}) %collective-permute-start) | collective-permute-done | bytes 1703968 | tf_op jit(solution)/shard_map/while/body/eval_jaxpr/ppermute | solution.py:15
  1381.3 33.4 %collective-permute-done.1 = bf16[2,2,832,256]{3,2,1,0:T(8,128)(2,1)} collective-permute-done((bf16[2,2,832,256]{3,2,1,0:T(8,128)(2,1)}, bf16[2,2,832,256]{3,2,1,0:T(8,128)(2,1)}, u32[]{:S(2)}, u32[]{:S(2)}) %collective-permute-start.1) | collective-permute-done | bytes 1703968 | tf_op jit(solution)/shard_map/while/body/eval_jaxpr/ppermute | solution.py:15
  1418.2 28.6 %collective-permute-done = bf16[2,2,832,256]{3,2,1,0:T(8,128)(2,1)} collective-permute-done((bf16[2,2,832,256]{3,2,1,0:T(8,128)(2,1)S(1)}, bf16[2,2,832,256]{3,2,1,0:T(8,128)(2,1)}, u32[]{:S(2)}, u32[]{:S(2)}) %collective-permute-start) | collective-permute-done | bytes 1703968 | tf_op jit(solution)/shard_map/while/body/eval_jaxpr/ppermute | solution.py:15
  1521.7 33.4 %collective-permute-done.1 = bf16[2,2,832,256]{3,2,1,0:T(8,128)(2,1)} collective-permute-done((bf16[2,2,832,256]{3,2,1,0:T(8,128)(2,1)}, bf16[2,2,832,256]{3,2,1,0:T(8,128)(2,1)}, u32[]{:S(2)}, u32[]{:S(2)}) %collective-permute-start.1) | collective-permute-done | bytes 1703968 | tf_op jit(solution)/shard_map/while/body/eval_jaxpr/ppermute | solution.py:15
  1558.5 27.7 %collective-permute-done = bf16[2,2,832,256]{3,2,1,0:T(8,128)(2,1)} collective-permute-done((bf16[2,2,832,256]{3,2,1,0:T(8,128)(2,1)S(1)}, bf16[2,2,832,256]{3,2,1,0:T(8,128)(2,1)}, u32[]{:S(2)}, u32[]{:S(2)}) %collective-permute-start) | collective-permute-done | bytes 1703968 | tf_op jit(solution)/shard_map/while/body/eval_jaxpr/ppermute | solution.py:15
  1661.1 33.4 %collective-permute-done.1 = bf16[2,2,832,256]{3,2,1,0:T(8,128)(2,1)} collective-permute-done((bf16[2,2,832,256]{3,2,1,0:T(8,128)(2,1)}, bf16[2,2,832,256]{3,2,1,0:T(8,128)(2,1)}, u32[]{:S(2)}, u32[]{:S(2)}) %collective-permute-start.1) | collective-permute-done | bytes 1703968 | tf_op jit(solution)/shard_map/while/body/eval_jaxpr/ppermute | solution.py:15
  1698.0 26.8 %collective-permute-done = bf16[2,2,832,256]{3,2,1,0:T(8,128)(2,1)} collective-permute-done((bf16[2,2,832,256]{3,2,1,0:T(8,128)(2,1)S(1)}, bf16[2,2,832,256]{3,2,1,0:T(8,128)(2,1)}, u32[]{:S(2)}, u32[]{:S(2)}) %collective-permute-start) | collective-permute-done | bytes 1703968 | tf_op jit(solution)/shard_map/while/body/eval_jaxpr/ppermute | solution.py:15
  1799.6 33.4 %collective-permute-done.1 = bf16[2,2,832,256]{3,2,1,0:T(8,128)(2,1)} collective-permute-done((bf16[2,2,832,256]{3,2,1,0:T(8,128)(2,1)}, bf16[2,2,832,256]{3,2,1,0:T(8,128)(2,1)}, u32[]{:S(2)}, u32[]{:S(2)}) %collective-permute-start.1) | collective-permute-done | bytes 1703968 | tf_op jit(solution)/shard_map/while/body/eval_jaxpr/ppermute | solution.py:15
  1836.5 25.9 %collective-permute-done = bf16[2,2,832,256]{3,2,1,0:T(8,128)(2,1)} collective-permute-done((bf16[2,2,832,256]{3,2,1,0:T(8,128)(2,1)S(1)}, bf16[2,2,832,256]{3,2,1,0:T(8,128)(2,1)}, u32[]{:S(2)}, u32[]{:S(2)}) %collective-permute-start) | collective-permute-done | bytes 1703968 | tf_op jit(solution)/shard_map/while/body/eval_jaxpr/ppermute | solution.py:15
  1902.6 191.6 %all-reduce.5.cloned.1.call-done = (bf16[1024,3,4,64]{0,3,2,1:T(8,128)(2,1)}, bf16[4,64,1024]{2,1,0:T(8,128)(2,1)}, bf16[1024,2,656]{0,2,1:T(8,128)(2,1)}, bf16[656,1024]{1,0:T(8,128)(2,1)}) async-done(((bf16[1024,3,4,64]{0,3,2,1:T(8,128)(2,1)}, bf16[4,64,1024]{2,1,0:T(8,128)(2,1)}, bf16[1024,2,656]{0,2,1:T(8,128)(2,1)}, bf16[656,1024]{1,0:T(8,128)(2,1)}), (bf16[1024,3,4,64]{0,3,2,1:T(8,128)(2,1)}, ...) | async-done | bytes 6127632 | tf_op jit(solution)/shard_map/psum | solution.py:215
  2104.2 31.2 %reduce-scatter.11.cloned.1.call-done = bf16[2,208,1024]{2,1,0:T(8,128)(2,1)} async-done(((bf16[2,832,1024]{2,1,0:T(8,128)(2,1)}), bf16[2,208,1024]{2,1,0:T(8,128)(2,1)}) %reduce-scatter.11.cloned.1.call-update) | async-done | bytes 851984 | tf_op jit(solution)/shard_map/reduce_scatter | solution.py:203
  2139.9 21.3 all-reduce.1
  (385 shorter events, 856.2 us)
Async XLA Ops:
  7.2 618.6 %copy-start = (bf16[1024,2,656]{0,2,1:T(8,128)(2,1)S(1)}, bf16[1024,2,656]{0,2,1:T(8,128)(2,1)}, u32[]{:S(2)}) copy-start(bf16[1024,2,656]{0,2,1:T(8,128)(2,1)} %param.16) | copy-start | bytes 8060932
  7.2 39.6 %all-gather.7.cloned.1.call-start = ((), (), s32[]{:S(2)}) async-start(), calls=%async_computation.4 | async-start | bytes 4259840 | tf_op jit(solution)/shard_map/all_gather | solution.py:71
  13.9 251.0 %all-gather.9.cloned.1.call-start = ((), (), s32[]{:S(2)}) async-start(), calls=%async_computation.5 | async-start | bytes 15335424 | tf_op jit(solution)/shard_map/all_gather | solution.py:91
  14.4 100.0 %copy-start.13 = (f32[832,64]{0,1:T(8,128)}, f32[832,64]{0,1:T(8,128)S(1)}, u32[]{:S(2)}) copy-start(f32[832,64]{0,1:T(8,128)S(1)} %get-tuple-element.391) | copy-start | bytes 638980
  14.4 100.0 %copy-start.19 = (f32[832,64]{0,1:T(8,128)}, f32[832,64]{0,1:T(8,128)S(1)}, u32[]{:S(2)}) copy-start(f32[832,64]{0,1:T(8,128)S(1)} %get-tuple-element.392) | copy-start | bytes 638980
  75.2 486.9 %reduce-scatter.5.cloned.1.call-start = ((), (), s32[]{:S(2)}) async-start(), calls=%async_computation.6 | async-start | bytes 4259840 | tf_op jit(solution)/shard_map/reduce_scatter | solution.py:104
  524.1 69.5 %all-gather.13.cloned.1.call-start = ((), (), s32[]{:S(2)}) async-start(), calls=%async_computation.9 | async-start | bytes 4259840 | tf_op jit(solution)/shard_map/all_gather | solution.py:126
  524.7 101.1 %all-gather.11.cloned.1.call-start = ((), (), s32[]{:S(2)}) async-start(), calls=%async_computation.7 | async-start | bytes 4259840 | tf_op jit(solution)/shard_map/all_gather | solution.py:114
  563.6 134.9 %copy-start.48 = (f32[2,208]{1,0:T(2,128)}, f32[2,208]{1,0:T(2,128)S(1)}, u32[]{:S(2)}) copy-start(f32[2,208]{1,0:T(2,128)S(1)} %broadcast_multiply_fusion.3) | copy-start | bytes 4996
  565.2 133.3 %copy-start.53 = (f32[2,208]{1,0:T(2,128)}, f32[2,208]{1,0:T(2,128)S(1)}, u32[]{:S(2)}) copy-start(f32[2,208]{1,0:T(2,128)S(1)} %fusion.96) | copy-start | bytes 4996
  566.6 128.5 %reduce-scatter.9.cloned.1.call-start = ((), (), s32[]{:S(2)}) async-start(), calls=%async_computation.10 | async-start | bytes 4259840 | tf_op jit(solution)/shard_map/reduce_scatter | solution.py:137
  655.3 75.2 %all-gather.15.cloned.1.call-start = ((), (), s32[]{:S(2)}) async-start(), calls=%async_computation.11 | async-start | bytes 4259840 | tf_op jit(solution)/shard_map/all_gather | solution.py:148
  700.3 1394.0 %all-reduce.5.cloned.1.call-start = ((), (), s32[]{:S(2)}) async-start(), calls=%async_computation.13 | async-start | bytes 12255232 | tf_op jit(solution)/shard_map/psum | solution.py:215
  800.9 43.0 %collective-permute-start.1 = (bf16[2,2,832,256]{3,2,1,0:T(8,128)(2,1)}, bf16[2,2,832,256]{3,2,1,0:T(8,128)(2,1)}, u32[]{:S(2)}, u32[]{:S(2)}) collective-permute-start(bf16[2,2,832,256]{3,2,1,0:T(8,128)(2,1)} %fusion.156), channel_id=1, source_target_pairs={{28,0},{0,4},{4,8},{8,12},{12,16},{16,20},{20,24},{24,28},{29,1},{... | collective-permute-start | bytes 5111816 | tf_op jit(solution)/shard_map/while/body/eval_jaxpr/ppermute | solution.py:15
  802.4 77.4 %collective-permute-start = (bf16[2,2,832,256]{3,2,1,0:T(8,128)(2,1)S(1)}, bf16[2,2,832,256]{3,2,1,0:T(8,128)(2,1)}, u32[]{:S(2)}, u32[]{:S(2)}) collective-permute-start(bf16[2,2,832,256]{3,2,1,0:T(8,128)(2,1)S(1)} %copy.131), channel_id=1, source_target_pairs={{28,0},{0,4},{4,8},{8,12},{12,16},{16,20},{20,24},{24,28},{29,1},{... | collective-permute-start | bytes 5111816 | tf_op jit(solution)/shard_map/while/body/eval_jaxpr/ppermute | solution.py:15
  944.9 43.2 %collective-permute-start.1 = (bf16[2,2,832,256]{3,2,1,0:T(8,128)(2,1)}, bf16[2,2,832,256]{3,2,1,0:T(8,128)(2,1)}, u32[]{:S(2)}, u32[]{:S(2)}) collective-permute-start(bf16[2,2,832,256]{3,2,1,0:T(8,128)(2,1)} %fusion.156), channel_id=1, source_target_pairs={{28,0},{0,4},{4,8},{8,12},{12,16},{16,20},{20,24},{24,28},{29,1},{... | collective-permute-start | bytes 5111816 | tf_op jit(solution)/shard_map/while/body/eval_jaxpr/ppermute | solution.py:15
  944.9 78.1 %collective-permute-start = (bf16[2,2,832,256]{3,2,1,0:T(8,128)(2,1)S(1)}, bf16[2,2,832,256]{3,2,1,0:T(8,128)(2,1)}, u32[]{:S(2)}, u32[]{:S(2)}) collective-permute-start(bf16[2,2,832,256]{3,2,1,0:T(8,128)(2,1)S(1)} %copy.131), channel_id=1, source_target_pairs={{28,0},{0,4},{4,8},{8,12},{12,16},{16,20},{20,24},{24,28},{29,1},{... | collective-permute-start | bytes 5111816 | tf_op jit(solution)/shard_map/while/body/eval_jaxpr/ppermute | solution.py:15
  1088.0 43.2 %collective-permute-start.1 = (bf16[2,2,832,256]{3,2,1,0:T(8,128)(2,1)}, bf16[2,2,832,256]{3,2,1,0:T(8,128)(2,1)}, u32[]{:S(2)}, u32[]{:S(2)}) collective-permute-start(bf16[2,2,832,256]{3,2,1,0:T(8,128)(2,1)} %fusion.156), channel_id=1, source_target_pairs={{28,0},{0,4},{4,8},{8,12},{12,16},{16,20},{20,24},{24,28},{29,1},{... | collective-permute-start | bytes 5111816 | tf_op jit(solution)/shard_map/while/body/eval_jaxpr/ppermute | solution.py:15
  1088.0 77.2 %collective-permute-start = (bf16[2,2,832,256]{3,2,1,0:T(8,128)(2,1)S(1)}, bf16[2,2,832,256]{3,2,1,0:T(8,128)(2,1)}, u32[]{:S(2)}, u32[]{:S(2)}) collective-permute-start(bf16[2,2,832,256]{3,2,1,0:T(8,128)(2,1)S(1)} %copy.131), channel_id=1, source_target_pairs={{28,0},{0,4},{4,8},{8,12},{12,16},{16,20},{20,24},{24,28},{29,1},{... | collective-permute-start | bytes 5111816 | tf_op jit(solution)/shard_map/while/body/eval_jaxpr/ppermute | solution.py:15
  1230.2 43.2 %collective-permute-start.1 = (bf16[2,2,832,256]{3,2,1,0:T(8,128)(2,1)}, bf16[2,2,832,256]{3,2,1,0:T(8,128)(2,1)}, u32[]{:S(2)}, u32[]{:S(2)}) collective-permute-start(bf16[2,2,832,256]{3,2,1,0:T(8,128)(2,1)} %fusion.156), channel_id=1, source_target_pairs={{28,0},{0,4},{4,8},{8,12},{12,16},{16,20},{20,24},{24,28},{29,1},{... | collective-permute-start | bytes 5111816 | tf_op jit(solution)/shard_map/while/body/eval_jaxpr/ppermute | solution.py:15
  1230.2 76.2 %collective-permute-start = (bf16[2,2,832,256]{3,2,1,0:T(8,128)(2,1)S(1)}, bf16[2,2,832,256]{3,2,1,0:T(8,128)(2,1)}, u32[]{:S(2)}, u32[]{:S(2)}) collective-permute-start(bf16[2,2,832,256]{3,2,1,0:T(8,128)(2,1)S(1)} %copy.131), channel_id=1, source_target_pairs={{28,0},{0,4},{4,8},{8,12},{12,16},{16,20},{20,24},{24,28},{29,1},{... | collective-permute-start | bytes 5111816 | tf_op jit(solution)/shard_map/while/body/eval_jaxpr/ppermute | solution.py:15
  1371.5 43.2 %collective-permute-start.1 = (bf16[2,2,832,256]{3,2,1,0:T(8,128)(2,1)}, bf16[2,2,832,256]{3,2,1,0:T(8,128)(2,1)}, u32[]{:S(2)}, u32[]{:S(2)}) collective-permute-start(bf16[2,2,832,256]{3,2,1,0:T(8,128)(2,1)} %fusion.156), channel_id=1, source_target_pairs={{28,0},{0,4},{4,8},{8,12},{12,16},{16,20},{20,24},{24,28},{29,1},{... | collective-permute-start | bytes 5111816 | tf_op jit(solution)/shard_map/while/body/eval_jaxpr/ppermute | solution.py:15
  1371.5 75.3 %collective-permute-start = (bf16[2,2,832,256]{3,2,1,0:T(8,128)(2,1)S(1)}, bf16[2,2,832,256]{3,2,1,0:T(8,128)(2,1)}, u32[]{:S(2)}, u32[]{:S(2)}) collective-permute-start(bf16[2,2,832,256]{3,2,1,0:T(8,128)(2,1)S(1)} %copy.131), channel_id=1, source_target_pairs={{28,0},{0,4},{4,8},{8,12},{12,16},{16,20},{20,24},{24,28},{29,1},{... | collective-permute-start | bytes 5111816 | tf_op jit(solution)/shard_map/while/body/eval_jaxpr/ppermute | solution.py:15
  1511.9 43.2 %collective-permute-start.1 = (bf16[2,2,832,256]{3,2,1,0:T(8,128)(2,1)}, bf16[2,2,832,256]{3,2,1,0:T(8,128)(2,1)}, u32[]{:S(2)}, u32[]{:S(2)}) collective-permute-start(bf16[2,2,832,256]{3,2,1,0:T(8,128)(2,1)} %fusion.156), channel_id=1, source_target_pairs={{28,0},{0,4},{4,8},{8,12},{12,16},{16,20},{20,24},{24,28},{29,1},{... | collective-permute-start | bytes 5111816 | tf_op jit(solution)/shard_map/while/body/eval_jaxpr/ppermute | solution.py:15
  1511.9 74.4 %collective-permute-start = (bf16[2,2,832,256]{3,2,1,0:T(8,128)(2,1)S(1)}, bf16[2,2,832,256]{3,2,1,0:T(8,128)(2,1)}, u32[]{:S(2)}, u32[]{:S(2)}) collective-permute-start(bf16[2,2,832,256]{3,2,1,0:T(8,128)(2,1)S(1)} %copy.131), channel_id=1, source_target_pairs={{28,0},{0,4},{4,8},{8,12},{12,16},{16,20},{20,24},{24,28},{29,1},{... | collective-permute-start | bytes 5111816 | tf_op jit(solution)/shard_map/while/body/eval_jaxpr/ppermute | solution.py:15
  1651.3 43.2 %collective-permute-start.1 = (bf16[2,2,832,256]{3,2,1,0:T(8,128)(2,1)}, bf16[2,2,832,256]{3,2,1,0:T(8,128)(2,1)}, u32[]{:S(2)}, u32[]{:S(2)}) collective-permute-start(bf16[2,2,832,256]{3,2,1,0:T(8,128)(2,1)} %fusion.156), channel_id=1, source_target_pairs={{28,0},{0,4},{4,8},{8,12},{12,16},{16,20},{20,24},{24,28},{29,1},{... | collective-permute-start | bytes 5111816 | tf_op jit(solution)/shard_map/while/body/eval_jaxpr/ppermute | solution.py:15
  1651.3 73.4 %collective-permute-start = (bf16[2,2,832,256]{3,2,1,0:T(8,128)(2,1)S(1)}, bf16[2,2,832,256]{3,2,1,0:T(8,128)(2,1)}, u32[]{:S(2)}, u32[]{:S(2)}) collective-permute-start(bf16[2,2,832,256]{3,2,1,0:T(8,128)(2,1)S(1)} %copy.131), channel_id=1, source_target_pairs={{28,0},{0,4},{4,8},{8,12},{12,16},{16,20},{20,24},{24,28},{29,1},{... | collective-permute-start | bytes 5111816 | tf_op jit(solution)/shard_map/while/body/eval_jaxpr/ppermute | solution.py:15
  1789.8 43.2 %collective-permute-start.1 = (bf16[2,2,832,256]{3,2,1,0:T(8,128)(2,1)}, bf16[2,2,832,256]{3,2,1,0:T(8,128)(2,1)}, u32[]{:S(2)}, u32[]{:S(2)}) collective-permute-start(bf16[2,2,832,256]{3,2,1,0:T(8,128)(2,1)} %fusion.156), channel_id=1, source_target_pairs={{28,0},{0,4},{4,8},{8,12},{12,16},{16,20},{20,24},{24,28},{29,1},{... | collective-permute-start | bytes 5111816 | tf_op jit(solution)/shard_map/while/body/eval_jaxpr/ppermute | solution.py:15
  1789.9 72.5 %collective-permute-start = (bf16[2,2,832,256]{3,2,1,0:T(8,128)(2,1)S(1)}, bf16[2,2,832,256]{3,2,1,0:T(8,128)(2,1)}, u32[]{:S(2)}, u32[]{:S(2)}) collective-permute-start(bf16[2,2,832,256]{3,2,1,0:T(8,128)(2,1)S(1)} %copy.131), channel_id=1, source_target_pairs={{28,0},{0,4},{4,8},{8,12},{12,16},{16,20},{20,24},{24,28},{29,1},{... | collective-permute-start | bytes 5111816 | tf_op jit(solution)/shard_map/while/body/eval_jaxpr/ppermute | solution.py:15
  1887.1 248.4 %reduce-scatter.11.cloned.1.call-start = ((), (), s32[]{:S(2)}) async-start(), calls=%async_computation.12 | async-start | bytes 4259840 | tf_op jit(solution)/shard_map/reduce_scatter | solution.py:203
  1895.3 282.5 %reduce-scatter.7.cloned.1.call-start = ((), (), s32[]{:S(2)}) async-start(), calls=%async_computation.8 | async-start | bytes 4259840 | tf_op jit(solution)/shard_map/reduce_scatter | solution.py:117
  2103.1 74.6 %copy-start.49 = (f32[2,208]{1,0:T(2,128)S(1)}, f32[2,208]{1,0:T(2,128)}, u32[]{:S(2)}) copy-start(f32[2,208]{1,0:T(2,128)} %copy-done.48) | copy-start | bytes 4996
  (69 other events, 888.7 us)
Sparse Core Ops, SparseCore 0:
  14.0 32.7 all-gather.6
  75.3 189.4 all-gather.8
  524.2 37.8 reduce-scatter.4
  563.6 30.0 all-gather.12
  595.7 30.0 all-gather.10
  655.4 39.6 reduce-scatter.8
  700.4 30.0 all-gather.14
  1887.2 206.9 all-reduce.4
  2096.9 38.4 reduce-scatter.10
  2137.8 39.8 reduce-scatter.6
where the time goes:
time: 2200 us; the launch traced here: 2190 us
  waiting for transfers between devices  1050 us (48%)
  matrix products  657 us (30%)
  other arithmetic  226 us (10%)
  local copies, waits for them, and re-layouts  179 us (8%)
  blocking collectives  59.7 us (3%)
    ppermute x16, waiting for transfers between devices, from_behind(): return lax.ppermute(block, axis, route)  496 us
    psum x1, waiting for transfers between devices, shards(): lax.psum(grad_qkv_w.astype(jnp.bfloat16), 'ctx').astype(jnp.float32)  192 us
    dot_general x9, matrix products, score_block(): jnp.einsum('sche,srhe->shcr', query, keys, preferred_element_type=jnp.flo...  170 us
    all_gather x1, waiting for transfers between devices, shards(): lax.all_gather(kv_pair, 'ctx', axis=2, tiled=True)  148 us
    dot_general x8, matrix products, back_block(): jnp.einsum('sche,srhe->shcr', d_attn, vals, preferred_element_type=jnp.fl...  123 us
    dot_general x8, matrix products, back_block(): jnp.einsum('shcr,sche->srhe', probs.astype(jnp.bfloat16), d_attn, preferr...  93 us
    reduce_sum x1, other arithmetic, shards(): run_sum = jnp.sum(weights, axis=-1)  77.8 us
    dot_general x8, matrix products, back_block(): jnp.einsum('shcr,srhe->sche', d_scores, keys, preferred_element_type=jnp....  77.5 us
  transfers between devices with their start and end apart: 26, of which 26 were waited for; matrix products, arithmetic and copies ran while one was open for 8% of the time, Pallas kernels for 0%

commit v1 on v0

v1 whole, which is shorter than its diff:
```python
import functools
import math

import jax
import jax.numpy as jnp
from jax import lax
from jax.experimental import pallas as pl
from jax.experimental.pallas import tpu as pltpu
from jax.sharding import PartitionSpec as P

theta_log = math.log(160000.0)
neg_fill = -1e30
safe_bound = 60.0
log2_e = math.log2(math.e)
wide_keys = 1664
fine_keys = 512
cut_count = 4
bf16 = jnp.bfloat16
f32 = jnp.float32
vmem_limit = 56 * 2**20


def swap(block, axis, bits):
    size = lax.axis_size(axis)
    return lax.ppermute(block, axis, [(i, i ^ bits) for i in range(size)])


def bit_list(size):
    bits, b = [], 1
    while b < size:
        bits.append(b)
        b *= 2
    return bits


def total(value, axis):
    for b in bit_list(lax.axis_size(axis)):
        value = value + swap(value, axis, b)
    return value


def gather_blocks(block):
    held = {0: block}
    for b in reversed(bit_list(lax.axis_size("tp"))):
        for j in list(held):
            held[j ^ b] = swap(held[j], "tp", b)
    return [held[j] for j in range(len(held))]


def scatter_blocks(blocks):
    held = dict(enumerate(blocks))
    for b in bit_list(lax.axis_size("tp")):
        for j in sorted(held):
            if j & b:
                got = swap(held.pop(j), "tp", b)
                summed = held[j ^ b].astype(f32) + got.astype(f32)
                held[j ^ b] = summed if len(held) == 1 else summed.astype(bf16)
    return held[0]


def dot(a, b, ca, cb):
    return lax.dot_general(a, b, (((ca,), (cb,)), ((), ())), preferred_element_type=f32)


def lanes():
    return lax.broadcasted_iota(jnp.int32, (1, 128), 1)


def rot(u):
    first = (lanes() & 63) < 32
    return jnp.where(first, -pltpu.roll(u, 96, 1), pltpu.roll(u, 32, 1))


def rot_back(w):
    first = (lanes() & 63) < 32
    return jnp.where(first, pltpu.roll(w, 96, 1), -pltpu.roll(w, 32, 1))


def call(kernel, ins, outs, scratch, smem_ins=1, grid=None, in_specs=None, out_specs=None):
    whole = pl.BlockSpec(memory_space=pltpu.VMEM)
    if in_specs is None:
        in_specs = [pl.BlockSpec(memory_space=pltpu.SMEM)] * smem_ins + [whole] * (
            len(ins) - smem_ins
        )
        out_specs = [whole] * len(outs)
    extra = {} if grid is None else {"grid": grid}
    return pl.pallas_call(
        kernel,
        in_specs=in_specs,
        out_specs=out_specs,
        out_shape=outs,
        scratch_shapes=scratch,
        compiler_params=pltpu.CompilerParams(vmem_limit_bytes=vmem_limit),
        **extra,
    )(*ins)


def assemble(meta, pieces, x_scr):
    part = pieces[0].shape[0]
    for j, piece in enumerate(pieces):
        at = pl.multiple_of((meta[2] ^ j) * part, 8)
        x_scr[pl.ds(at, part), :] = piece[...].astype(f32)


def disperse(meta, x_scr, pieces):
    part = pieces[0].shape[0]
    for j, piece in enumerate(pieces):
        at = pl.multiple_of((meta[2] ^ j) * part, 8)
        piece[...] = x_scr[pl.ds(at, part), :].astype(bf16)


def qkv_kernel(heads, tp, half, scale, meta, *refs):
    pieces, refs = refs[:tp], refs[tp:]
    weight, ck, sk, cd, sd, x_ref, *refs = refs
    kv_outs, q_outs, (x_scr, kv_scr, q_scr) = refs[:heads], refs[heads : 2 * heads], refs[-3:]
    assemble(meta, pieces, x_scr)
    x = x_scr[...].astype(bf16)
    x_ref[...] = x
    left = lanes() < 64
    for h in range(heads):
        both = dot(x, weight[:, h * 256 : (h + 1) * 256], 1, 0)
        kv = both[:, :128]
        q = both[:, 128:]
        kv_scr[h] = (kv * ck[...] + rot(kv) * sk[...]).astype(bf16)
        q = (q * cd[...] + rot(q) * sd[...]) * scale
        q_scr[h] = jnp.where(left, q[:half], q[half:]).astype(bf16)
    for kh in range(heads):
        kv_outs[kh][...] = kv_scr[meta[1] ^ kh]
        q_outs[kh][...] = q_scr[meta[1] ^ kh]


def row_range(tok, meta, length):
    low = jnp.zeros_like(tok)
    high = jnp.full_like(tok, length)
    for d in range(cut_count):
        c = meta[3 + d]
        low = jnp.where(tok >= c, jnp.maximum(low, c), low)
        high = jnp.where(tok < c, jnp.minimum(high, c), high)
    return low, high


def load_keys(meta, ctx, rows, kv_refs, kvs, vx, sems):
    copies = []
    for k in range(ctx):
        at = pl.multiple_of((meta[0] ^ k) * rows, rows)
        copies.append(pltpu.make_async_copy(kv_refs[k], kvs.at[pl.ds(at, rows)], sems.at[k]))
    for c in copies:
        c.start()
    for c in copies:
        c.wait()
    vx[...] = jnp.where(lanes() < 64, jnp.ones((), bf16), kvs[...])


def attn_fwd_kernel(heads, ctx, rows, length, meta, *refs):
    q_refs, refs = refs[:heads], refs[heads:]
    kv_refs, refs = refs[:ctx], refs[ctx:]
    o_refs, refs = refs[:heads], refs[heads:]
    linv_ref, m_ref, kvs, vx, q_scr, qc, acc, m_scr, norms, sems = refs
    half = rows // 2
    i = pl.program_id(0)
    left = lanes() < 64

    @pl.when(i == 0)
    def _():
        load_keys(meta, ctx, rows, kv_refs, kvs, vx, sems)
        k = jnp.where(left, kvs[...].astype(f32), 0.0)
        norms[0] = jnp.max(jnp.sum(k * k, axis=1, keepdims=True))
        for c in range(heads):
            q_scr[c] = q_refs[c][...]

    q = q_scr[i].astype(f32)
    qa = jnp.where(left, q, 0.0)
    qb = jnp.where(left, pltpu.roll(q, 64, 1), 0.0)
    qc[:half] = qa.astype(bf16)
    qc[half:] = qb.astype(bf16)
    q_norm = jnp.max(jnp.sum(jnp.maximum(qa * qa, qb * qb), axis=1, keepdims=True))
    safe = q_norm * norms[0] < safe_bound * safe_bound
    single = meta[3] >= length
    fast = jnp.logical_and(safe, single)
    acc[...] = jnp.zeros_like(acc)
    m_scr[...] = jnp.zeros_like(m_scr)

    @pl.when(fast)
    def _():
        def step(j, _):
            keys = pl.ds(pl.multiple_of(j * wide_keys, wide_keys), wide_keys)
            e = jnp.exp2(dot(qc[...], kvs[keys, :], 1, 1)).astype(bf16)
            acc[...] += dot(e, vx[keys, :], 1, 0)
            return 0

        lax.fori_loop(0, length // wide_keys, step, 0)

    @pl.when(jnp.logical_not(fast))
    def _():
        first = (meta[0] ^ (i * (ctx // heads))) * rows
        tok = first + lax.broadcasted_iota(jnp.int32, (rows, 1), 0)
        low, high = row_range(tok, meta, length)
        j_low = lax.div(row_range(first, meta, length)[0], fine_keys)
        j_high = lax.div(row_range(first + rows - 1, meta, length)[1] + fine_keys - 1, fine_keys)

        def masked(j):
            keys = pl.ds(pl.multiple_of(j * fine_keys, fine_keys), fine_keys)
            spot = j * fine_keys + lax.broadcasted_iota(jnp.int32, (1, fine_keys), 1)
            allowed = jnp.logical_and(spot >= low, spot < high)
            return keys, allowed, dot(qc[...], kvs[keys, :], 1, 1)

        @pl.when(jnp.logical_not(safe))
        def _():
            m_scr[...] = jnp.full_like(m_scr, neg_fill)

            def peak(j, _):
                _, allowed, s = masked(j)
                s = jnp.max(jnp.where(allowed, s, neg_fill), axis=1, keepdims=True)
                m_scr[...] = jnp.maximum(m_scr[...], s)
                return 0

            lax.fori_loop(j_low, j_high, peak, 0)

        def step(j, _):
            keys, allowed, s = masked(j)
            e = jnp.where(allowed, jnp.exp2(s - m_scr[:, 0:1]), 0.0).astype(bf16)
            acc[...] += dot(e, vx[keys, :], 1, 0)
            return 0

        lax.fori_loop(j_low, j_high, step, 0)

    a = acc[...]
    o = a / pltpu.roll(a, 64, 1)
    out = jnp.where(left, pltpu.roll(o[:half], 64, 1), o[half:]).astype(bf16)
    for c in range(heads):

        @pl.when(i == c)
        def _(c=c):
            o_refs[c][...] = out

    inv = 1.0 / a
    linv_ref[...] = jnp.where(left, inv[:half], pltpu.roll(inv[half:], 64, 1))
    m_ref[...] = jnp.where(left, m_scr[:half], m_scr[half:])


def attn_bwd_kernel(heads, ctx, rows, length, meta, *refs):
    q_refs, refs = refs[:heads], refs[heads:]
    do_refs, refs = refs[:heads], refs[heads:]
    o_refs, refs = refs[:heads], refs[heads:]
    linv_ref, m_ref, *refs = refs
    kv_refs, refs = refs[:ctx], refs[ctx:]
    dq_refs, refs = refs[:heads], refs[heads:]
    dkv_refs, refs = refs[:ctx], refs[ctx:]
    kvs, vx, q_scr, do_scr, o_scr, qc, dc, qt, dt, dq_acc, dkv_t, dkv_n, sems = refs
    half = rows // 2
    i = pl.program_id(0)
    lane = lanes()
    left = lane < 64

    @pl.when(i == 0)
    def _():
        load_keys(meta, ctx, rows, kv_refs, kvs, vx, sems)
        dkv_t[...] = jnp.zeros_like(dkv_t)
        for c in range(heads):
            q_scr[c] = q_refs[c][...]
            do_scr[c] = do_refs[c][...]
            o_scr[c] = o_refs[c][...]

    q = q_scr[i].astype(f32)
    do = do_scr[i].astype(f32) * linv_ref[...]
    prod = do * o_scr[i].astype(f32)
    delta_a = jnp.sum(jnp.where(left, prod, 0.0), axis=1, keepdims=True)
    delta_b = jnp.sum(jnp.where(left, 0.0, prod), axis=1, keepdims=True)

    def extended(x, delta):
        coarse = delta.astype(bf16).astype(f32)
        ends = jnp.where(lane == 0, -coarse, jnp.where(lane == 1, coarse - delta, 0.0))
        return jnp.where(left, ends, x).astype(bf16)

    qc[:half] = jnp.where(left, q, 0.0).astype(bf16)
    qc[half:] = jnp.where(left, pltpu.roll(q, 64, 1), 0.0).astype(bf16)
    dc[:half] = extended(pltpu.roll(do, 64, 1), delta_a)
    dc[half:] = extended(do, delta_b)
    qt[...] = qc[...].astype(f32).T[:64].astype(bf16)
    dt[...] = dc[...].astype(f32).T[64:].astype(bf16)
    dq_acc[...] = jnp.zeros_like(dq_acc)
    shift = m_ref[...]
    shifted = jnp.max(jnp.abs(shift)) > 0.0
    single = meta[3] >= length
    fast = jnp.logical_and(single, jnp.logical_not(shifted))

    def accumulate(keys, e, allowed):
        ds = e * dot(dc[...], vx[keys, :], 1, 1)
        if allowed is not None:
            ds = jnp.where(allowed, ds, 0.0)
        ds = ds.astype(bf16)
        e = e.astype(bf16)
        dq_acc[...] += dot(ds, kvs[keys, :], 1, 0)
        dkv_t[:64, keys] += dot(qt[...], ds, 1, 0)
        dkv_t[64:, keys] += dot(dt[...], e, 1, 0)

    @pl.when(fast)
    def _():
        def step(j, _):
            keys = pl.ds(pl.multiple_of(j * wide_keys, wide_keys), wide_keys)
            accumulate(keys, jnp.exp2(dot(qc[...], kvs[keys, :], 1, 1)), None)
            return 0

        lax.fori_loop(0, length // wide_keys, step, 0)

    @pl.when(jnp.logical_not(fast))
    def _():
        first = (meta[0] ^ (i * (ctx // heads))) * rows
        tok = first + lax.broadcasted_iota(jnp.int32, (rows, 1), 0)
        low, high = row_range(tok, meta, length)
        j_low = lax.div(row_range(first, meta, length)[0], fine_keys)
        j_high = lax.div(row_range(first + rows - 1, meta, length)[1] + fine_keys - 1, fine_keys)
        m = jnp.concatenate([shift[:, 0:1], shift[:, 64:65]], axis=0)

        def step(j, _):
            keys = pl.ds(pl.multiple_of(j * fine_keys, fine_keys), fine_keys)
            spot = j * fine_keys + lax.broadcasted_iota(jnp.int32, (1, fine_keys), 1)
            allowed = jnp.logical_and(spot >= low, spot < high)
            s = dot(qc[...], kvs[keys, :], 1, 1)
            e = jnp.where(allowed, jnp.exp2(s - m), 0.0)
            accumulate(keys, e, allowed)
            return 0

        lax.fori_loop(j_low, j_high, step, 0)

    a = dq_acc[...] * 0.125
    out = jnp.where(left, a[:half], pltpu.roll(a[half:], 64, 1)).astype(bf16)
    for c in range(heads):

        @pl.when(i == c)
        def _(c=c):
            dq_refs[c][...] = out

    @pl.when(i == heads - 1)
    def _():
        is_key = lax.broadcasted_iota(jnp.int32, (128, 1), 0) < 64
        for j in range(length // wide_keys):
            part = dkv_t[:, j * wide_keys : (j + 1) * wide_keys]
            part = jnp.where(is_key, part * math.log(2.0), part)
            dkv_n[j * wide_keys : (j + 1) * wide_keys, :] = part.T.astype(bf16)
        copies = []
        for k in range(ctx):
            at = pl.multiple_of((meta[0] ^ k) * rows, rows)
            copies.append(
                pltpu.make_async_copy(dkv_n.at[pl.ds(at, rows)], dkv_refs[k], sems.at[k])
            )
        for c in copies:
            c.start()
        for c in copies:
            c.wait()


def proj_kernel(heads, tp, meta, *refs):
    o_refs, refs = refs[:heads], refs[heads:]
    weight, o_nat, *refs = refs
    pieces, (o_scr, x_scr) = refs[:tp], refs[tp:]
    half = o_refs[0].shape[0]
    left = lanes() < 64
    for kh in range(heads):
        o_scr[meta[1] ^ kh] = o_refs[kh][...]
    zero = jnp.zeros((), bf16)
    for h in range(heads):
        o = o_scr[h]
        o_nat[:half, h * 128 : (h + 1) * 128] = jnp.where(left, o, zero)
        o_nat[half:, h * 128 : (h + 1) * 128] = jnp.where(left, zero, o)
    x_scr[...] = dot(o_nat[...], weight[...], 1, 0)
    disperse(meta, x_scr, pieces)


def d_attn_kernel(heads, tp, meta, *refs):
    pieces, refs = refs[:tp], refs[tp:]
    weight, full, *refs = refs
    outs, (x_scr, d_scr) = refs[:heads], refs[heads:]
    half = outs[0].shape[0]
    left = lanes() < 64
    assemble(meta, pieces, x_scr)
    x = x_scr[...].astype(bf16)
    full[...] = x
    for h in range(heads):
        d = dot(x, weight[h * 128 : (h + 1) * 128, :], 1, 1)
        d_scr[h] = jnp.where(left, d[:half], d[half:]).astype(bf16)
    for kh in range(heads):
        outs[kh][...] = d_scr[meta[1] ^ kh]


def d_qkv_kernel(heads, ctx, tp, meta, *refs):
    dkv_refs, refs = refs[:ctx], refs[ctx:]
    dq_refs, refs = refs[:heads], refs[heads:]
    weight, ck, sk, cd, sd, d_all, *refs = refs
    pieces, (kv_scr, q_scr, x_scr) = refs[:tp], refs[tp:]
    half = dq_refs[0].shape[0]
    parts = ctx // heads
    left = lanes() < 64
    for kh in range(heads):
        z = dkv_refs[kh * parts][...].astype(f32)
        for kp in range(1, parts):
            z = z + dkv_refs[kh * parts + kp][...].astype(f32)
        kv_scr[meta[1] ^ kh] = (z * ck[...] + rot_back(z * sk[...])).astype(bf16)
        q_scr[meta[1] ^ kh] = dq_refs[kh][...]
    for h in range(heads):
        d_all[:, h * 256 : h * 256 + 128] = kv_scr[h]
        d = q_scr[h].astype(f32)
        d = jnp.concatenate([jnp.where(left, d, 0.0), jnp.where(left, 0.0, d)], axis=0)
        d = d * cd[...] + rot_back(d * sd[...])
        d_all[:, h * 256 + 128 : (h + 1) * 256] = d.astype(bf16)
    x_scr[...] = dot(d_all[...], weight[...], 1, 1)
    disperse(meta, x_scr, pieces)


def rope_tables(positions, width):
    freqs = jnp.exp(-(2.0 * jnp.arange(width // 2, dtype=f32) / width) * theta_log)
    angles = positions.astype(f32)[:, None] * freqs[None, :]
    cosine, sine = jnp.cos(angles), jnp.sin(angles)
    one, none = jnp.ones_like(angles), jnp.zeros_like(angles)
    lay = lambda *parts: jnp.concatenate(parts, axis=1)
    return (
        lay(cosine, cosine, one, one),
        lay(sine, sine, none, none),
        lay(cosine, cosine, cosine, cosine),
        lay(sine, sine, sine, sine),
    )


def layer_norm(rows, gain):
    mean = jnp.mean(rows, axis=-1, keepdims=True)
    cent = rows - mean
    var = jnp.mean(cent * cent, axis=-1, keepdims=True)
    return cent * lax.rsqrt(var + 1e-05) * gain


def shards(
    hidden_in,
    norm1_gain,
    qkv_weight,
    attn_weight,
    norm2_gain,
    ffn_in_weight,
    ffn_out_weight,
    doc_ids,
    out_grad,
):
    seqs = hidden_in.shape[0]
    width = hidden_in.shape[2]
    heads = qkv_weight.shape[2]
    head_dim = qkv_weight.shape[3]
    rows = doc_ids.shape[1]
    half = rows // 2
    ff = ffn_out_weight.shape[0]
    ctx, tp = lax.axis_size("ctx"), lax.axis_size("tp")
    parts = ctx // heads
    length = ctx * rows
    own = rows // tp
    me, spot = lax.axis_index("ctx"), lax.axis_index("tp")
    sds = jax.ShapeDtypeStruct

    steps = jnp.arange(1, cut_count + 1, dtype=jnp.int32)
    counts = jnp.sum((doc_ids[:, :, None] < steps).astype(f32), axis=1)
    cuts = total(counts, "ctx").astype(jnp.int32)
    place = jnp.stack([me, me // parts, spot]).astype(jnp.int32)
    metas = [jnp.concatenate([place, cuts[s]]) for s in range(seqs)]

    wq, wk, wv = qkv_weight[:, 0], qkv_weight[:, 1], qkv_weight[:, 2]
    w_all = jnp.concatenate([wk, wv, wq, wq], axis=2).reshape(width, heads * 256)
    w_out = jnp.concatenate([attn_weight, attn_weight], axis=1).reshape(heads * 128, width)
    w_in = ffn_in_weight.reshape(width, 2 * ff)
    tables = rope_tables(me * rows + jnp.arange(rows, dtype=jnp.int32), head_dim)
    scale = log2_e / math.sqrt(head_dim)

    resid = [hidden_in[s].astype(f32) for s in range(seqs)]
    full1, q_got, kv_got = [], [], []
    for s in range(seqs):
        blocks = gather_blocks(layer_norm(resid[s], norm1_gain).astype(bf16))
        outs = call(
            functools.partial(qkv_kernel, heads, tp, half, scale),
            [metas[s], *blocks, w_all, *tables],
            [sds((rows, width), bf16)]
            + [sds((rows, 128), bf16)] * heads
            + [sds((half, 128), bf16)] * heads,
            [
                pltpu.VMEM((rows, width), f32),
                pltpu.VMEM((heads, rows, 128), bf16),
                pltpu.VMEM((heads, half, 128), bf16),
            ],
        )
        full1.append(outs[0])
        kv, q = outs[1 : 1 + heads], outs[1 + heads :]
        q_got.append([q[0]] + [swap(q[h], "ctx", h * parts) for h in range(1, heads)])
        kv_got.append(
            [kv[0]] + [swap(kv[k // parts], "ctx", k) for k in range(1, ctx)]
        )

    smem = pl.BlockSpec(memory_space=pltpu.SMEM)
    hbm = pl.BlockSpec(memory_space=pl.ANY)
    small = pl.BlockSpec((half, 128), lambda i: (0, 0))
    tile = pl.BlockSpec((half, 128), lambda i: (i, 0))
    o_mine, linv, shift, o_nat, mid, grads_full = [], [], [], [], [], []
    for s in range(seqs):
        outs = call(
            functools.partial(attn_fwd_kernel, heads, ctx, rows, length),
            [metas[s], *q_got[s], *kv_got[s]],
            [sds((half, 128), bf16)] * heads + [sds((heads * half, 128), f32)] * 2,
            [
                pltpu.VMEM((length, 128), bf16),
                pltpu.VMEM((length, 128), bf16),
                pltpu.VMEM((heads, half, 128), bf16),
                pltpu.VMEM((rows, 128), bf16),
                pltpu.VMEM((rows, 128), f32),
                pltpu.VMEM((rows, 128), f32),
                pltpu.SMEM((1,), f32),
                pltpu.SemaphoreType.DMA((ctx,)),
            ],
            grid=(heads,),
            in_specs=[smem] + [small] * heads + [hbm] * ctx,
            out_specs=[small] * heads + [tile, tile],
        )
        o_mine.append(outs[:heads])
        linv.append(outs[heads])
        shift.append(outs[heads + 1])
        back = [outs[0]] + [swap(outs[h], "ctx", h * parts) for h in range(1, heads)]
        outs = call(
            functools.partial(proj_kernel, heads, tp),
            [metas[s], *back, w_out],
            [sds((rows, heads * 128), bf16)] + [sds((own, width), bf16)] * tp,
            [pltpu.VMEM((heads, half, 128), bf16), pltpu.VMEM((rows, width), f32)],
        )
        o_nat.append(outs[0])
        mid.append(resid[s] + scatter_blocks(outs[1:]))
        grads_full.append(jnp.concatenate(gather_blocks(out_grad[s]), axis=0))

    block_out, d_mid, dmid_full, d_attn, gain2 = [], [], [], [], 0.0
    g_out_w, g_in_w, g_attn_w = 0.0, 0.0, 0.0
    for s in range(seqs):
        normed2, pull_norm2 = jax.vjp(layer_norm, mid[s], norm2_gain)
        full2 = jnp.concatenate(gather_blocks(normed2.astype(bf16)), axis=0)
        upper = dot(full2, w_in, 1, 0)
        first, second = upper[:, :ff], upper[:, ff:]
        gated, pull_gelu = jax.vjp(
            lambda a, b: jax.nn.gelu(a, approximate=False) * b, first, second
        )
        act = gated.astype(bf16)
        d_act = dot(grads_full[s], ffn_out_weight, 1, 1)
        d_upper = jnp.concatenate(pull_gelu(d_act), axis=1).astype(bf16)
        d_part = dot(d_upper, w_in, 1, 1).astype(bf16)
        d_normed2 = scatter_blocks([d_part[j * own : (j + 1) * own] for j in range(tp)])
        d_mid_norm, d_gain = pull_norm2(d_normed2)
        gain2 = gain2 + d_gain
        d_mid.append(out_grad[s].astype(f32) + d_mid_norm)
        pieces = gather_blocks(d_mid[s].astype(bf16))
        outs = call(
            functools.partial(d_attn_kernel, heads, tp),
            [metas[s], *pieces, w_out],
            [sds((rows, width), bf16)] + [sds((half, 128), bf16)] * heads,
            [pltpu.VMEM((rows, width), f32), pltpu.VMEM((heads, half, 128), bf16)],
        )
        dmid_full.append(outs[0])
        d = outs[1:]
        d_attn.append([d[0]] + [swap(d[h], "ctx", h * parts) for h in range(1, heads)])
        out_part = dot(act, ffn_out_weight, 1, 0).astype(bf16)
        ffn_sum = scatter_blocks([out_part[j * own : (j + 1) * own] for j in range(tp)])
        block_out.append((mid[s] + ffn_sum).astype(bf16))
        g_out_w = g_out_w + dot(act, grads_full[s], 0, 0)
        g_in_w = g_in_w + dot(full2, d_upper, 0, 0)
        g_attn_w = g_attn_w + dot(o_nat[s], dmid_full[s], 0, 0)
    g_attn_w = jnp.sum(g_attn_w.reshape(heads, 2, head_dim, width), axis=1)
    early = [lax.psum(g.astype(bf16), "ctx").astype(f32) for g in (g_out_w, g_in_w, g_attn_w)]

    d_all, in_grad, gain1 = [], [], 0.0
    for s in range(seqs):
        outs = call(
            functools.partial(attn_bwd_kernel, heads, ctx, rows, length),
            [metas[s], *q_got[s], *d_attn[s], *o_mine[s], linv[s], shift[s], *kv_got[s]],
            [sds((half, 128), bf16)] * heads + [sds((rows, 128), bf16)] * ctx,
            [
                pltpu.VMEM((length, 128), bf16),
                pltpu.VMEM((length, 128), bf16),
                pltpu.VMEM((heads, half, 128), bf16),
                pltpu.VMEM((heads, half, 128), bf16),
                pltpu.VMEM((heads, half, 128), bf16),
                pltpu.VMEM((rows, 128), bf16),
                pltpu.VMEM((rows, 128), bf16),
                pltpu.VMEM((64, rows), bf16),
                pltpu.VMEM((64, rows), bf16),
                pltpu.VMEM((rows, 128), f32),
                pltpu.VMEM((128, length), f32),
                pltpu.VMEM((length, 128), bf16),
                pltpu.SemaphoreType.DMA((ctx,)),
            ],
            grid=(heads,),
            in_specs=[smem] + [small] * (3 * heads) + [tile, tile] + [hbm] * ctx,
            out_specs=[small] * heads + [hbm] * ctx,
        )
        dq = [outs[0]] + [swap(outs[h], "ctx", h * parts) for h in range(1, heads)]
        dkv = outs[heads:]
        dkv = [dkv[0]] + [swap(dkv[k], "ctx", k) for k in range(1, ctx)]
        outs = call(
            functools.partial(d_qkv_kernel, heads, ctx, tp),
            [metas[s], *dkv, *dq, w_all, *tables],
            [sds((rows, heads * 256), bf16)] + [sds((own, width), bf16)] * tp,
            [
                pltpu.VMEM((heads, rows, 128), bf16),
                pltpu.VMEM((heads, half, 128), bf16),
                pltpu.VMEM((rows, width), f32),
            ],
        )
        d_all.append(outs[0])
        _, pull_norm1 = jax.vjp(layer_norm, resid[s], norm1_gain)
        d_in_norm, d_gain = pull_norm1(scatter_blocks(outs[1:]))
        gain1 = gain1 + d_gain
        in_grad.append((d_mid[s] + d_in_norm).astype(bf16))
    g_qkv_w = sum(dot(full1[s], d_all[s], 0, 0) for s in range(seqs))
    g_qkv_w = g_qkv_w.reshape(width, heads, 4, head_dim)
    g_qkv_w = jnp.stack(
        [g_qkv_w[:, :, 2] + g_qkv_w[:, :, 3], g_qkv_w[:, :, 0], g_qkv_w[:, :, 1]], axis=1
    )
    g_qkv_w = lax.psum(g_qkv_w.astype(bf16), "ctx").astype(f32)
    gains = total(total(jnp.stack([gain1, gain2]), "tp"), "ctx")
    return (
        jnp.stack(block_out),
        jnp.stack(in_grad),
        gains[0],
        g_qkv_w,
        early[2],
        gains[1],
        early[1].reshape(width, 2, ff),
        early[0],
    )


def solution(mesh):
    in_specs = (
        P(None, ("ctx", "tp"), None),
        P(),
        P(None, None, "tp", None),
        P("tp", None, None),
        P(),
        P(None, None, "tp"),
        P("tp", None),
        P(None, "ctx"),
        P(None, ("ctx", "tp"), None),
    )
    out_specs = (
        P(None, ("ctx", "tp"), None),
        P(None, ("ctx", "tp"), None),
        P(),
        P(None, None, "tp", None),
        P("tp", None, None),
        P(),
        P(None, None, "tp"),
        P("tp", None),
    )
    return jax.shard_map(shards, mesh=mesh, in_specs=in_specs, out_specs=out_specs, check_vma=False)
```

time: 2200 us -> 916 us (0.42)
  waiting for transfers between devices: 1050 us -> 335 us
  matrix products: 657 us -> 75.8 us
  starting transfers between devices: 4.55 us -> 215 us
  Pallas kernels: 0 us -> 208 us
  other arithmetic: 226 us -> 45.8 us
  local copies, waits for them, and re-layouts: 179 us -> 13.8 us
  blocking collectives: 59.7 us -> 0 us
    dot_general x54 -> x16, matrix products: 657 us -> 75.8 us  [dot(): lax.dot_general(a, b, (((ca,), (cb,)), ((), ())), preferred_element_type=...]
    ppermute x16 -> x108, waiting for transfers between devices: 496 us -> 170 us  [swap(): return lax.ppermute(block, axis, [(i, i ^ bits) for i in range(size)])]
    all_gather x5 -> x0, waiting for transfers between devices: 242 us -> none  [the longest x1 148 us: shards(): lax.all_gather(kv_pair, 'ctx', axis=2, tiled=True)]
    ppermute x16 -> x108, starting transfers between devices: 4.14 us -> 215 us  [swap(): return lax.ppermute(block, axis, [(i, i ^ bits) for i in range(size)])]
    pallas_call x0 -> x12, Pallas kernels: none -> 208 us  [call(): pl.pallas_call(kernel, in_specs=in_specs, out_specs=out_specs, out_shape=...]
    reduce_scatter x4 -> x0, waiting for transfers between devices: 116 us -> none  [the longest x1 39.7 us: shards(): lax.psum_scatter(jnp.einsum('scgf,dgf->scd', d_upper, ffn_in_weight, pref...]
    slice x32 -> x5, local copies, waits for them, and re-layouts: 86.5 us -> 0.83 us  [the longest x1 0.61 us: shards(): gains[1]]
    convert_element_type x27 -> x16, other arithmetic: 89.4 us -> 12 us  [the longest x8 4.2 us: scatter_blocks(): held[j ^ b] = summed if len(held) == 1 else summed.astype(bf16)]
  transfers between devices with their start and end apart: 26 -> 109, of which waited for: 26 -> 32; matrix products, arithmetic and copies ran while one was open for 8% -> 10% of each run, Pallas kernels for 0% -> 22%
where the time goes in v1:
time: 916 us; the launch traced here: 910 us
  waiting for transfers between devices  335 us (37%)
  starting transfers between devices  215 us (23%)
  Pallas kernels  208 us (23%)
  matrix products  75.8 us (8%)
  other arithmetic  45.8 us (5%)
  between operations  15.8 us (2%)
  local copies, waits for them, and re-layouts  13.8 us (2%)
    ppermute x108, starting transfers between devices, swap(): return lax.ppermute(block, axis, [(i, i ^ bits) for i in range(size)])  215 us
    pallas_call x12, Pallas kernels, call(): pl.pallas_call(kernel, in_specs=in_specs, out_specs=out_specs, out_shape=...  208 us
    ppermute x108, waiting for transfers between devices, swap(): return lax.ppermute(block, axis, [(i, i ^ bits) for i in range(size)])  170 us
    psum x1, waiting for transfers between devices, shards(): g_qkv_w = lax.psum(g_qkv_w.astype(bf16), 'ctx').astype(f32)  165 us
    dot_general x16, matrix products, dot(): lax.dot_general(a, b, (((ca,), (cb,)), ((), ())), preferred_element_type=...  75.8 us
  transfers between devices with their start and end apart: 109, of which 32 were waited for; matrix products, arithmetic and copies ran while one was open for 10% of the time, Pallas kernels for 22%

profile of v1, /device:TPU:0, one launch (start us, length us, event | category | flops | bytes accessed | tf_op | source)
XLA Modules:
  0.0 909.8 jit_solution(2543730726214653616)
XLA Ops:
  74.2 6.5 shard_map.152
  81.4 11.6 %collective-permute-done.37.refs_8_.refs_18_ = bf16[832,128]{1,0:T(8,128)(2,1)S(1)} collective-permute-done((bf16[832,128]{1,0:T(8,128)(2,1)}, bf16[832,128]{1,0:T(8,128)(2,1)S(1)}, u32[]{:S(2)}, u32[]{:S(2)}) %collective-permute-start.37) | collective-permute-done | bytes 213024 | tf_op jit(solution)/shard_map/ppermute | solution.py:25
  98.1 7.7 collective-permute-start.7
  106.5 33.7 %shard_map.156 = (bf16[416,128]{1,0:T(8,128)(2,1)}, bf16[416,128]{1,0:T(8,128)(2,1)}, bf16[416,128]{1,0:T(8,128)(2,1)}, bf16[416,128]{1,0:T(8,128)(2,1)}, f32[1664,128]{1,0:T(8,128)}, /*index=5*/f32[1664,128]{1,0:T(8,128)}) custom-call(s32[7]{0:T(128)} %pad_add_fusion.2.meta, bf16[416,128]{1,0:T(8,128)(2,1)} %get-tuple-element.108.refs_0_, ...), custom_call_target="tpu_custom_call" | custom-call | tf_op jit(solution)/shard_map/pallas_call | solution.py:87
  163.0 29.7 %collective-permute-start.45 = (bf16[208,1024]{1,0:T(8,128)(2,1)}, bf16[208,1024]{1,0:T(8,128)(2,1)S(1)}, u32[]{:S(2)}, u32[]{:S(2)}) collective-permute-start(bf16[208,1024]{1,0:T(8,128)(2,1)} %get-tuple-element.123), channel_id=1, source_target_pairs={{0,1},{1,0},{2,3},{3,2},{4,5},{5,4},{6,7},{7,6},{8,9},{9,8},{10,11... | collective-permute-start | bytes 1277960 | tf_op jit(solution)/shard_map/ppermute | solution.py:25
  193.6 24.4 %shard_map.153 = (bf16[416,128]{1,0:T(8,128)(2,1)}, bf16[416,128]{1,0:T(8,128)(2,1)}, bf16[416,128]{1,0:T(8,128)(2,1)}, bf16[416,128]{1,0:T(8,128)(2,1)}, f32[1664,128]{1,0:T(8,128)}, /*index=5*/f32[1664,128]{1,0:T(8,128)}) custom-call(s32[7]{0:T(128)} %get-tuple-element.208.meta, bf16[416,128]{1,0:T(8,128)(2,1)} %get-tuple-element.92.refs_0_, ...), custom_call_target="tpu_custom_call" | custom-call | tf_op jit(solution)/shard_map/pallas_call | solution.py:87
  231.9 20.2 %collective-permute-start.20 = (bf16[208,1024]{1,0:T(8,128)(2,1)}, bf16[208,1024]{1,0:T(8,128)(2,1)S(1)}, u32[]{:S(2)}, u32[]{:S(2)}) collective-permute-start(bf16[208,1024]{1,0:T(8,128)(2,1)} %get-tuple-element.107), channel_id=1, source_target_pairs={{0,1},{1,0},{2,3},{3,2},{4,5},{5,4},{6,7},{7,6},{8,9},{9,8},{10,11... | collective-permute-start | bytes 1277960 | tf_op jit(solution)/shard_map/ppermute | solution.py:25
  256.1 9.4 %collective-permute-done.46 = bf16[208,1024]{1,0:T(8,128)(2,1)S(1)} collective-permute-done((bf16[208,1024]{1,0:T(8,128)(2,1)S(1)}, bf16[208,1024]{1,0:T(8,128)(2,1)S(1)}, u32[]{:S(2)}, u32[]{:S(2)}) %collective-permute-start.46) | collective-permute-done | bytes 426016 | tf_op jit(solution)/shard_map/ppermute | solution.py:25
  265.5 8.3 collective-permute-done.21
  277.0 10.6 %collective-permute-done.48 = bf16[208,1024]{1,0:T(8,128)(2,1)S(1)} collective-permute-done((bf16[208,1024]{1,0:T(8,128)(2,1)S(1)}, bf16[208,1024]{1,0:T(8,128)(2,1)S(1)}, u32[]{:S(2)}, u32[]{:S(2)}) %collective-permute-start.48) | collective-permute-done | bytes 426016 | tf_op jit(solution)/shard_map/ppermute | solution.py:25
  288.1 6.8 collective-permute-done.79
  298.0 7.3 add_convert_fusion.2
  313.9 16.8 %collective-permute-done.83 = bf16[208,1024]{1,0:T(8,128)(2,1)S(1)} collective-permute-done((bf16[208,1024]{1,0:T(8,128)(2,1)S(1)}, bf16[208,1024]{1,0:T(8,128)(2,1)S(1)}, u32[]{:S(2)}, u32[]{:S(2)}) %collective-permute-start.83) | collective-permute-done | bytes 426016 | tf_op jit(solution)/shard_map/ppermute | solution.py:25
  332.6 9.7 %collective-permute-done.23 = bf16[208,1024]{1,0:T(8,128)(2,1)S(1)} collective-permute-done((bf16[208,1024]{1,0:T(8,128)(2,1)S(1)}, bf16[208,1024]{1,0:T(8,128)(2,1)S(1)}, u32[]{:S(2)}, u32[]{:S(2)}) %collective-permute-start.23) | collective-permute-done | bytes 426016 | tf_op jit(solution)/shard_map/ppermute | solution.py:25
  347.2 9.9 %add_convert_fusion.3 = (bf16[832,656]{1,0:T(8,128)(2,1)}, f32[832,656]{1,0:T(8,128)S(1)}, f32[832,656]{1,0:T(8,128)S(1)}) fusion(f32[832,1312]{1,0:T(8,128)S(1)} %fusion.57, bf16[656,1024]{1,0:T(8,128)(2,1)S(1)} %copy-done.90, bf16[208,1024]{1,0:T(8,128)(2,1)S(1)} %collective-permute-done.55, bf16[208,1024]{1,0:T(8,128)(2,1)S(1)} %collective-permute-done.54, ...), kind=kOutput, calls=%fused_computation.9 | convolution fusion | flops 1164440576 | bytes 12871680 | tf_op jit(solution)/shard_map/dot_general | solution.py:62
  368.0 9.5 %collective-permute-done.58 = bf16[208,1024]{1,0:T(8,128)(2,1)S(1)} collective-permute-done((bf16[208,1024]{1,0:T(8,128)(2,1)S(1)}, bf16[208,1024]{1,0:T(8,128)(2,1)S(1)}, u32[]{:S(2)}, u32[]{:S(2)}) %collective-permute-start.58) | collective-permute-done | bytes 426016 | tf_op jit(solution)/shard_map/ppermute | solution.py:25
  379.2 7.0 collective-permute-done.27
  390.4 10.2 %collective-permute-done.85.refs_2_ = bf16[208,1024]{1,0:T(8,128)(2,1)S(1)} collective-permute-done((bf16[208,1024]{1,0:T(8,128)(2,1)S(1)}, bf16[208,1024]{1,0:T(8,128)(2,1)S(1)}, u32[]{:S(2)}, u32[]{:S(2)}) %collective-permute-start.85) | collective-permute-done | bytes 426016 | tf_op jit(solution)/shard_map/ppermute | solution.py:25
  400.6 7.8 collective-permute-done.60.refs_2_
  408.4 7.2 fusion.14
  439.0 8.6 add_convert_fusion
  448.3 61.6 %shard_map.162 = (bf16[416,128]{1,0:T(8,128)(2,1)}, bf16[416,128]{1,0:T(8,128)(2,1)}, bf16[416,128]{1,0:T(8,128)(2,1)}, bf16[416,128]{1,0:T(8,128)(2,1)}, bf16[8...) custom-call(s32[7]{0:T(128)} %pad_add_fusion.2.meta, ...), custom_call_target="tpu_custom_call" | custom-call | tf_op jit(solution)/shard_map/pallas_call | solution.py:87
  509.9 12.2 %collective-permute-start.90 = (bf16[832,128]{1,0:T(8,128)(2,1)}, bf16[832,128]{1,0:T(8,128)(2,1)S(1)}, u32[]{:S(2)}, u32[]{:S(2)}) collective-permute-start(bf16[832,128]{1,0:T(8,128)(2,1)} %get-tuple-element.153), channel_id=1, source_target_pairs={{0,4},{4,0},{8,12},{12,8},{16,20},{20,16},{24,28},{28,24},{1,5},{5... | collective-permute-start | bytes 638984 | tf_op jit(solution)/shard_map/ppermute | solution.py:25
  542.5 43.6 %shard_map.159 = (bf16[416,128]{1,0:T(8,128)(2,1)}, bf16[416,128]{1,0:T(8,128)(2,1)}, bf16[416,128]{1,0:T(8,128)(2,1)}, bf16[416,128]{1,0:T(8,128)(2,1)}, bf16[8...) custom-call(s32[7]{0:T(128)} %get-tuple-element.208.meta, ...), custom_call_target="tpu_custom_call" | custom-call | tf_op jit(solution)/shard_map/pallas_call | solution.py:87
  586.2 16.2 %collective-permute-start.65 = (bf16[832,128]{1,0:T(8,128)(2,1)}, bf16[832,128]{1,0:T(8,128)(2,1)S(1)}, u32[]{:S(2)}, u32[]{:S(2)}) collective-permute-start(bf16[832,128]{1,0:T(8,128)(2,1)} %get-tuple-element.131), channel_id=1, source_target_pairs={{0,4},{4,0},{8,12},{12,8},{16,20},{20,16},{24,28},{28,24},{1,5},{5... | collective-permute-start | bytes 638984 | tf_op jit(solution)/shard_map/ppermute | solution.py:25
  613.9 7.6 shard_map.163
  636.4 10.4 %collective-permute-done.69.refs_5_ = bf16[832,128]{1,0:T(8,128)(2,1)S(1)} collective-permute-done((bf16[832,128]{1,0:T(8,128)(2,1)S(1)}, bf16[832,128]{1,0:T(8,128)(2,1)S(1)}, u32[]{:S(2)}, u32[]{:S(2)}) %collective-permute-start.69) | collective-permute-done | bytes 213024 | tf_op jit(solution)/shard_map/ppermute | solution.py:25
  647.7 7.5 shard_map.160
  662.4 18.1 %collective-permute-start.101 = (bf16[208,1024]{1,0:T(8,128)(2,1)}, bf16[208,1024]{1,0:T(8,128)(2,1)S(1)}, u32[]{:S(2)}, u32[]{:S(2)}) collective-permute-start(bf16[208,1024]{1,0:T(8,128)(2,1)} %get-tuple-element.167), channel_id=1, source_target_pairs={{0,1},{1,0},{2,3},{3,2},{4,5},{5,4},{6,7},{7,6},{8,9},{9,8},{10,11... | collective-permute-start | bytes 1277960 | tf_op jit(solution)/shard_map/ppermute | solution.py:25
  687.6 8.4 collective-permute-done.102
  696.0 8.6 collective-permute-done.77
  727.5 165.2 %all-reduce.3.cloned.1.call-done = (bf16[1024,3,4,64]{0,3,2,1:T(8,128)(2,1)}, bf16[4,64,1024]{2,1,0:T(8,128)(2,1)}, bf16[1024,2,656]{0,2,1:T(8,128)(2,1)}, bf16[656,1024]{1,0:T(8,128)(2,1)}) async-done(((bf16[1024,3,4,64]{0,3,2,1:T(8,128)(2,1)}, bf16[4,64,1024]{2,1,0:T(8,128)(2,1)}, bf16[1024,2,656]{0,2,1:T(8,128)(2,1)}, bf16[656,1024]{1,0:T(8,128)(2,1)}), (bf16[1024,3,4,64]{0,3,2,1:T(8,128)(2,1)}, ...) | async-done | bytes 6127632 | tf_op jit(solution)/shard_map/psum | solution.py:615
  (542 shorter events, 271.7 us)
Async XLA Ops:
  7.2 885.5 %all-reduce.3.cloned.1.call-start = ((), (), s32[]{:S(2)}) async-start(), calls=%async_computation | async-start | bytes 12255232 | tf_op jit(solution)/shard_map/psum | solution.py:615
  13.1 28.3 %collective-permute-start.29 = (bf16[208,1024]{1,0:T(8,128)(2,1)}, bf16[208,1024]{1,0:T(8,128)(2,1)}, u32[]{:S(2)}, u32[]{:S(2)}) collective-permute-start(bf16[208,1024]{1,0:T(8,128)(2,1)} %get-tuple-element.232.refs_0_), channel_id=1, source_target_pairs={{0,2},{1,3},{2,0},{3,1},{4,6},{5,7},{6,4},{7,5},{8,10},{9,11},{10,... | collective-permute-start | bytes 1277960 | tf_op jit(solution)/shard_map/ppermute | solution.py:25
  16.1 27.1 %collective-permute-start.28 = (bf16[208,1024]{1,0:T(8,128)(2,1)}, bf16[208,1024]{1,0:T(8,128)(2,1)}, u32[]{:S(2)}, u32[]{:S(2)}) collective-permute-start(bf16[208,1024]{1,0:T(8,128)(2,1)} %get-tuple-element.232.refs_0_), channel_id=1, source_target_pairs={{0,1},{1,0},{2,3},{3,2},{4,5},{5,4},{6,7},{7,6},{8,9},{9,8},{10,11... | collective-permute-start | bytes 1277960 | tf_op jit(solution)/shard_map/ppermute | solution.py:25
  16.2 36.8 %collective-permute-start.3 = (bf16[208,1024]{1,0:T(8,128)(2,1)}, bf16[208,1024]{1,0:T(8,128)(2,1)}, u32[]{:S(2)}, u32[]{:S(2)}) collective-permute-start(bf16[208,1024]{1,0:T(8,128)(2,1)} %get-tuple-element.231.refs_0_), channel_id=1, source_target_pairs={{0,1},{1,0},{2,3},{3,2},{4,5},{5,4},{6,7},{7,6},{8,9},{9,8},{10,11... | collective-permute-start | bytes 1277960 | tf_op jit(solution)/shard_map/ppermute | solution.py:25
  64.3 28.7 %collective-permute-start.37 = (bf16[832,128]{1,0:T(8,128)(2,1)}, bf16[832,128]{1,0:T(8,128)(2,1)S(1)}, u32[]{:S(2)}, u32[]{:S(2)}) collective-permute-start(bf16[832,128]{1,0:T(8,128)(2,1)} %get-tuple-element.114), channel_id=1, source_target_pairs={{0,16},{4,20},{8,24},{12,28},{16,0},{20,4},{24,8},{28,12},{1,17},{... | collective-permute-start | bytes 638984 | tf_op jit(solution)/shard_map/ppermute | solution.py:25
  69.4 28.7 %collective-permute-start.38 = (bf16[832,128]{1,0:T(8,128)(2,1)}, bf16[832,128]{1,0:T(8,128)(2,1)S(1)}, u32[]{:S(2)}, u32[]{:S(2)}) collective-permute-start(bf16[832,128]{1,0:T(8,128)(2,1)} %get-tuple-element.114), channel_id=1, source_target_pairs={{0,20},{4,16},{8,28},{12,24},{16,4},{20,0},{24,12},{28,8},{1,21},{... | collective-permute-start | bytes 638984 | tf_op jit(solution)/shard_map/ppermute | solution.py:25
  69.5 28.6 %collective-permute-start.39 = (bf16[832,128]{1,0:T(8,128)(2,1)}, bf16[832,128]{1,0:T(8,128)(2,1)S(1)}, u32[]{:S(2)}, u32[]{:S(2)}) collective-permute-start(bf16[832,128]{1,0:T(8,128)(2,1)} %get-tuple-element.115), channel_id=1, source_target_pairs={{0,24},{4,28},{8,16},{12,20},{16,8},{20,12},{24,0},{28,4},{1,25},{... | collective-permute-start | bytes 638984 | tf_op jit(solution)/shard_map/ppermute | solution.py:25
  71.9 34.0 %collective-permute-start.40 = (bf16[832,128]{1,0:T(8,128)(2,1)}, bf16[832,128]{1,0:T(8,128)(2,1)S(1)}, u32[]{:S(2)}, u32[]{:S(2)}) collective-permute-start(bf16[832,128]{1,0:T(8,128)(2,1)} %get-tuple-element.115), channel_id=1, source_target_pairs={{0,28},{4,24},{8,20},{12,16},{16,12},{20,8},{24,4},{28,0},{1,29},{... | collective-permute-start | bytes 638984 | tf_op jit(solution)/shard_map/ppermute | solution.py:25
  80.8 66.9 %collective-permute-start.9 = (bf16[832,128]{1,0:T(8,128)(2,1)}, bf16[832,128]{1,0:T(8,128)(2,1)S(1)}, u32[]{:S(2)}, u32[]{:S(2)}) collective-permute-start(bf16[832,128]{1,0:T(8,128)(2,1)} %get-tuple-element.96.refs_4_.refs_14_), channel_id=1, source_target_pairs={{0,4},{4,0},{8,12},{12,8},{16,20},{20,16},{24,28},{28,24},{1,5},{5... | collective-permute-start | bytes 638984 | tf_op jit(solution)/shard_map/ppermute | solution.py:25
  93.1 56.5 %collective-permute-start.10 = (bf16[832,128]{1,0:T(8,128)(2,1)}, bf16[832,128]{1,0:T(8,128)(2,1)S(1)}, u32[]{:S(2)}, u32[]{:S(2)}) collective-permute-start(bf16[832,128]{1,0:T(8,128)(2,1)} %get-tuple-element.97), channel_id=1, source_target_pairs={{0,8},{4,12},{8,0},{12,4},{16,24},{20,28},{24,16},{28,20},{1,9},{5... | collective-permute-start | bytes 638984 | tf_op jit(solution)/shard_map/ppermute | solution.py:25
  98.1 42.2 %collective-permute-start.6 = (bf16[416,128]{1,0:T(8,128)(2,1)}, bf16[416,128]{1,0:T(8,128)(2,1)S(1)}, u32[]{:S(2)}, u32[]{:S(2)}) collective-permute-start(bf16[416,128]{1,0:T(8,128)(2,1)} %get-tuple-element.93), channel_id=1, source_target_pairs={{0,8},{4,12},{8,0},{12,4},{16,24},{20,28},{24,16},{28,20},{1,9},{5... | collective-permute-start | bytes 319496 | tf_op jit(solution)/shard_map/ppermute | solution.py:25
  98.1 47.2 %collective-permute-start.7 = (bf16[416,128]{1,0:T(8,128)(2,1)}, bf16[416,128]{1,0:T(8,128)(2,1)S(1)}, u32[]{:S(2)}, u32[]{:S(2)}) collective-permute-start(bf16[416,128]{1,0:T(8,128)(2,1)} %get-tuple-element.94), channel_id=1, source_target_pairs={{0,16},{4,20},{8,24},{12,28},{16,0},{20,4},{24,8},{28,12},{1,17},{... | collective-permute-start | bytes 319496 | tf_op jit(solution)/shard_map/ppermute | solution.py:25
  105.9 39.6 %collective-permute-start.8 = (bf16[416,128]{1,0:T(8,128)(2,1)}, bf16[416,128]{1,0:T(8,128)(2,1)S(1)}, u32[]{:S(2)}, u32[]{:S(2)}) collective-permute-start(bf16[416,128]{1,0:T(8,128)(2,1)} %get-tuple-element.95), channel_id=1, source_target_pairs={{0,24},{4,28},{8,16},{12,20},{16,8},{20,12},{24,0},{28,4},{1,25},{... | collective-permute-start | bytes 319496 | tf_op jit(solution)/shard_map/ppermute | solution.py:25
  149.6 43.1 %collective-permute-start.12 = (bf16[832,128]{1,0:T(8,128)(2,1)}, bf16[832,128]{1,0:T(8,128)(2,1)S(1)}, u32[]{:S(2)}, u32[]{:S(2)}) collective-permute-start(bf16[832,128]{1,0:T(8,128)(2,1)} %get-tuple-element.98), channel_id=1, source_target_pairs={{0,16},{4,20},{8,24},{12,28},{16,0},{20,4},{24,8},{28,12},{1,17},{... | collective-permute-start | bytes 638984 | tf_op jit(solution)/shard_map/ppermute | solution.py:25
  151.4 41.3 %collective-permute-start.13 = (bf16[832,128]{1,0:T(8,128)(2,1)}, bf16[832,128]{1,0:T(8,128)(2,1)S(1)}, u32[]{:S(2)}, u32[]{:S(2)}) collective-permute-start(bf16[832,128]{1,0:T(8,128)(2,1)} %get-tuple-element.98), channel_id=1, source_target_pairs={{0,20},{4,16},{8,28},{12,24},{16,4},{20,0},{24,12},{28,8},{1,21},{... | collective-permute-start | bytes 638984 | tf_op jit(solution)/shard_map/ppermute | solution.py:25
  153.2 39.5 %collective-permute-start.14 = (bf16[832,128]{1,0:T(8,128)(2,1)}, bf16[832,128]{1,0:T(8,128)(2,1)S(1)}, u32[]{:S(2)}, u32[]{:S(2)}) collective-permute-start(bf16[832,128]{1,0:T(8,128)(2,1)} %get-tuple-element.99), channel_id=1, source_target_pairs={{0,24},{4,28},{8,16},{12,20},{16,8},{20,12},{24,0},{28,4},{1,25},{... | collective-permute-start | bytes 638984 | tf_op jit(solution)/shard_map/ppermute | solution.py:25
  154.9 37.8 %collective-permute-start.15 = (bf16[832,128]{1,0:T(8,128)(2,1)}, bf16[832,128]{1,0:T(8,128)(2,1)S(1)}, u32[]{:S(2)}, u32[]{:S(2)}) collective-permute-start(bf16[832,128]{1,0:T(8,128)(2,1)} %get-tuple-element.99), channel_id=1, source_target_pairs={{0,28},{4,24},{8,20},{12,16},{16,12},{20,8},{24,4},{28,0},{1,29},{... | collective-permute-start | bytes 638984 | tf_op jit(solution)/shard_map/ppermute | solution.py:25
  163.0 89.5 %collective-permute-start.45 = (bf16[208,1024]{1,0:T(8,128)(2,1)}, bf16[208,1024]{1,0:T(8,128)(2,1)S(1)}, u32[]{:S(2)}, u32[]{:S(2)}) collective-permute-start(bf16[208,1024]{1,0:T(8,128)(2,1)} %get-tuple-element.123), channel_id=1, source_target_pairs={{0,1},{1,0},{2,3},{3,2},{4,5},{5,4},{6,7},{7,6},{8,9},{9,8},{10,11... | collective-permute-start | bytes 1277960 | tf_op jit(solution)/shard_map/ppermute | solution.py:25
  309.8 33.1 %collective-permute-start.54 = (bf16[208,1024]{1,0:T(8,128)(2,1)S(1)}, bf16[208,1024]{1,0:T(8,128)(2,1)S(1)}, u32[]{:S(2)}, u32[]{:S(2)}) collective-permute-start(bf16[208,1024]{1,0:T(8,128)(2,1)S(1)} %get-tuple-element.239), channel_id=1, source_target_pairs={{0,2},{1,3},{2,0},{3,1},{4,6},{5,7},{6,4},{7,5},{8,10},{9,11},{10,... | collective-permute-start | bytes 1277960 | tf_op jit(solution)/shard_map/ppermute | solution.py:25
  389.9 25.7 %collective-permute-start.84 = (bf16[208,1024]{1,0:T(8,128)(2,1)S(1)}, bf16[208,1024]{1,0:T(8,128)(2,1)S(1)}, u32[]{:S(2)}, u32[]{:S(2)}) collective-permute-start(bf16[208,1024]{1,0:T(8,128)(2,1)S(1)} %get-tuple-element.235.refs_0_), channel_id=1, source_target_pairs={{0,1},{1,0},{2,3},{3,2},{4,5},{5,4},{6,7},{7,6},{8,9},{9,8},{10,11... | collective-permute-start | bytes 1277960 | tf_op jit(solution)/shard_map/ppermute | solution.py:25
  389.9 40.0 %collective-permute-start.59 = (bf16[208,1024]{1,0:T(8,128)(2,1)S(1)}, bf16[208,1024]{1,0:T(8,128)(2,1)}, u32[]{:S(2)}, u32[]{:S(2)}) collective-permute-start(bf16[208,1024]{1,0:T(8,128)(2,1)S(1)} %get-tuple-element.236.refs_0_), channel_id=1, source_target_pairs={{0,1},{1,0},{2,3},{3,2},{4,5},{5,4},{6,7},{7,6},{8,9},{9,8},{10,11... | collective-permute-start | bytes 1277960 | tf_op jit(solution)/shard_map/ppermute | solution.py:25
  434.6 87.5 %collective-permute-start.62 = (bf16[416,128]{1,0:T(8,128)(2,1)}, bf16[416,128]{1,0:T(8,128)(2,1)S(1)}, u32[]{:S(2)}, u32[]{:S(2)}) collective-permute-start(bf16[416,128]{1,0:T(8,128)(2,1)} %get-tuple-element.125), channel_id=1, source_target_pairs={{0,8},{4,12},{8,0},{12,4},{16,24},{20,28},{24,16},{28,20},{1,9},{5... | collective-permute-start | bytes 319496 | tf_op jit(solution)/shard_map/ppermute | solution.py:25
  435.3 88.8 %collective-permute-start.63 = (bf16[416,128]{1,0:T(8,128)(2,1)}, bf16[416,128]{1,0:T(8,128)(2,1)S(1)}, u32[]{:S(2)}, u32[]{:S(2)}) collective-permute-start(bf16[416,128]{1,0:T(8,128)(2,1)} %get-tuple-element.126), channel_id=1, source_target_pairs={{0,16},{4,20},{8,24},{12,28},{16,0},{20,4},{24,8},{28,12},{1,17},{... | collective-permute-start | bytes 319496 | tf_op jit(solution)/shard_map/ppermute | solution.py:25
  437.2 87.6 %collective-permute-start.64 = (bf16[416,128]{1,0:T(8,128)(2,1)}, bf16[416,128]{1,0:T(8,128)(2,1)S(1)}, u32[]{:S(2)}, u32[]{:S(2)}) collective-permute-start(bf16[416,128]{1,0:T(8,128)(2,1)} %get-tuple-element.127), channel_id=1, source_target_pairs={{0,24},{4,28},{8,16},{12,20},{16,8},{20,12},{24,0},{28,4},{1,25},{... | collective-permute-start | bytes 319496 | tf_op jit(solution)/shard_map/ppermute | solution.py:25
  509.9 26.4 %collective-permute-start.90 = (bf16[832,128]{1,0:T(8,128)(2,1)}, bf16[832,128]{1,0:T(8,128)(2,1)S(1)}, u32[]{:S(2)}, u32[]{:S(2)}) collective-permute-start(bf16[832,128]{1,0:T(8,128)(2,1)} %get-tuple-element.153), channel_id=1, source_target_pairs={{0,4},{4,0},{8,12},{12,8},{16,20},{20,16},{24,28},{28,24},{1,5},{5... | collective-permute-start | bytes 638984 | tf_op jit(solution)/shard_map/ppermute | solution.py:25
  531.3 54.9 %collective-permute-start.92 = (bf16[832,128]{1,0:T(8,128)(2,1)}, bf16[832,128]{1,0:T(8,128)(2,1)S(1)}, u32[]{:S(2)}, u32[]{:S(2)}) collective-permute-start(bf16[832,128]{1,0:T(8,128)(2,1)} %get-tuple-element.155), channel_id=1, source_target_pairs={{0,12},{4,8},{8,4},{12,0},{16,28},{20,24},{24,20},{28,16},{1,13},{... | collective-permute-start | bytes 638984 | tf_op jit(solution)/shard_map/ppermute | solution.py:25
  532.2 70.2 %collective-permute-start.93 = (bf16[832,128]{1,0:T(8,128)(2,1)}, bf16[832,128]{1,0:T(8,128)(2,1)S(1)}, u32[]{:S(2)}, u32[]{:S(2)}) collective-permute-start(bf16[832,128]{1,0:T(8,128)(2,1)} %get-tuple-element.156), channel_id=1, source_target_pairs={{0,16},{4,20},{8,24},{12,28},{16,0},{20,4},{24,8},{28,12},{1,17},{... | collective-permute-start | bytes 638984 | tf_op jit(solution)/shard_map/ppermute | solution.py:25
  533.5 69.0 %collective-permute-start.94 = (bf16[832,128]{1,0:T(8,128)(2,1)}, bf16[832,128]{1,0:T(8,128)(2,1)S(1)}, u32[]{:S(2)}, u32[]{:S(2)}) collective-permute-start(bf16[832,128]{1,0:T(8,128)(2,1)} %get-tuple-element.157), channel_id=1, source_target_pairs={{0,20},{4,16},{8,28},{12,24},{16,4},{20,0},{24,12},{28,8},{1,21},{... | collective-permute-start | bytes 638984 | tf_op jit(solution)/shard_map/ppermute | solution.py:25
  536.2 68.2 %collective-permute-start.95 = (bf16[832,128]{1,0:T(8,128)(2,1)}, bf16[832,128]{1,0:T(8,128)(2,1)S(1)}, u32[]{:S(2)}, u32[]{:S(2)}) collective-permute-start(bf16[832,128]{1,0:T(8,128)(2,1)} %get-tuple-element.158), channel_id=1, source_target_pairs={{0,24},{4,28},{8,16},{12,20},{16,8},{20,12},{24,0},{28,4},{1,25},{... | collective-permute-start | bytes 638984 | tf_op jit(solution)/shard_map/ppermute | solution.py:25
  538.3 66.8 %collective-permute-start.96 = (bf16[832,128]{1,0:T(8,128)(2,1)}, bf16[832,128]{1,0:T(8,128)(2,1)S(1)}, u32[]{:S(2)}, u32[]{:S(2)}) collective-permute-start(bf16[832,128]{1,0:T(8,128)(2,1)} %get-tuple-element.159), channel_id=1, source_target_pairs={{0,28},{4,24},{8,20},{12,16},{16,12},{20,8},{24,4},{28,0},{1,29},{... | collective-permute-start | bytes 638984 | tf_op jit(solution)/shard_map/ppermute | solution.py:25
  586.2 40.8 %collective-permute-start.65 = (bf16[832,128]{1,0:T(8,128)(2,1)}, bf16[832,128]{1,0:T(8,128)(2,1)S(1)}, u32[]{:S(2)}, u32[]{:S(2)}) collective-permute-start(bf16[832,128]{1,0:T(8,128)(2,1)} %get-tuple-element.131), channel_id=1, source_target_pairs={{0,4},{4,0},{8,12},{12,8},{16,20},{20,16},{24,28},{28,24},{1,5},{5... | collective-permute-start | bytes 638984 | tf_op jit(solution)/shard_map/ppermute | solution.py:25
  602.4 26.7 %collective-permute-start.66 = (bf16[832,128]{1,0:T(8,128)(2,1)}, bf16[832,128]{1,0:T(8,128)(2,1)S(1)}, u32[]{:S(2)}, u32[]{:S(2)}) collective-permute-start(bf16[832,128]{1,0:T(8,128)(2,1)} %get-tuple-element.132), channel_id=1, source_target_pairs={{0,8},{4,12},{8,0},{12,4},{16,24},{20,28},{24,16},{28,20},{1,9},{5... | collective-permute-start | bytes 638984 | tf_op jit(solution)/shard_map/ppermute | solution.py:25
  (199 other events, 3404.3 us)
Sparse Core Ops, SparseCore 0:
  662.5 230.2 all-reduce.2
